TPU v7x, 32 devices: a whole 2x2x4 slice. The times are simulated.
32 devices in a mesh: section: 4 (over y, x), expert: 8 (over z, core).
Axes of the slice: x: 2, y: 2, z: 4, core: 2. Of those that a mesh axis runs over, the one named last changes fastest.
Arguments:
- layer_input: bfloat16 [4, 128, 4096], P('section', 'expert'), may hold values from -6 to 6
- w_gate: bfloat16 [4, 4096, 16384], P('section', None, 'expert'), may hold values from -0.09375 to 0.09375
- w_up: bfloat16 [4, 4096, 16384], P('section', None, 'expert'), may hold values from -0.09375 to 0.09375
- w_down: bfloat16 [4, 16384, 4096], P('section', 'expert'), may hold values from -0.1875 to 0.1875
- grad_out: bfloat16 [4, 128, 4096], P('section', 'expert'), may hold values from -1.5 to 1.5
- expert_ids: int32 [4, 128, 8], P('section', 'expert'), may hold values from 0 to 15, all different within a row; in each aligned block of 16 rows (0 to 15, 16 to 31, ..., all dimensions but the last counted through in order) at most 12 rows name the same one
- gates: bfloat16 [4, 128, 8], P('section', 'expert'), may hold values from 0.049804688 to 1
Outputs:
- grad_prev: bfloat16 [4, 128, 4096], P('section', 'expert')
- grad_w_gate: bfloat16 [4, 4096, 16384], P('section', None, 'expert')
- grad_w_up: bfloat16 [4, 4096, 16384], P('section', None, 'expert')
- grad_w_down: bfloat16 [4, 16384, 4096], P('section', 'expert')
Inputs may be any that keep to these rules, and one draw needn't show every extreme that they name: `expert_ids`: each token names 8 different experts; among the 16 tokens of one index of expert (aligned blocks of rows), no expert is named more than 12 times, a bound that some block reaches.
All inputs are finite; a program needn't handle non-finite values.
Results may differ from a plain program's by a relative error of at most 0.0065.
Values may be sent and summed in bfloat16 or wider, within the bound.
No kernel may reach another device: no remote copies, remote signals or barrier semaphores. Data moves between devices by JAX's collectives and lax.ppermute only.
A program may use at most 192 MiB of HBM per device.

v0:
```python
import functools

import jax
import jax.numpy as jnp
from jax import lax
from jax.experimental import pallas as pl
from jax.experimental.pallas import tpu as pltpu
from jax.sharding import PartitionSpec as P

EXPERTS = 16
LANES = 128
BF16, F32 = jnp.bfloat16, jnp.float32
MIB = 1 << 20


def contract(left, right, left_dim, right_dim):
    return lax.dot_general(
        left, right, (((left_dim,), (right_dim,)), ((), ())), preferred_element_type=F32
    )


def swap(block, bits):
    devices = lax.axis_size("expert")
    return lax.ppermute(block, "expert", [(i, i ^ bits) for i in range(devices)])


def across(block):
    devices = lax.axis_size("expert")
    found = {0: block}
    bits = devices // 2
    while bits > 1:
        found |= {mask | bits: swap(part, bits) for mask, part in found.items()}
        bits //= 2
    return found


def gather(block):
    near = across(block)
    masks = sorted(near)
    return [near[m] for m in masks] + [swap(near[m], 1) for m in masks]


def params(limit):
    return pltpu.CompilerParams(vmem_limit_bytes=limit * MIB)


def cost(flops, moved):
    return pl.CostEstimate(flops=flops, bytes_accessed=moved, transcendentals=0)


def joined(refs):
    return jnp.concatenate([r[...] for r in refs], axis=0) if len(refs) > 1 else refs[0][...]


def pre_kernel(count, *refs):
    pieces, (gate_ref, up_ref, x_ref, a_ref, b_ref) = refs[:count], refs[count:]

    @pl.when(pl.program_id(0) == 0)
    def _():
        a_ref[...] = jnp.zeros_like(a_ref)
        b_ref[...] = jnp.zeros_like(b_ref)

    x = joined(pieces)
    x_ref[...] = x
    a_ref[...] += jnp.dot(x, gate_ref[...], preferred_element_type=F32)
    b_ref[...] += jnp.dot(x, up_ref[...], preferred_element_type=F32)


def pre(pieces, w_gate, w_up):
    width, columns = w_gate.shape
    tokens = sum(p.shape[0] for p in pieces)
    depth = min(512, width)
    return pl.pallas_call(
        functools.partial(pre_kernel, len(pieces)),
        grid=(width // depth,),
        in_specs=[pl.BlockSpec((p.shape[0], depth), lambda i: (0, i)) for p in pieces]
        + [pl.BlockSpec((depth, columns), lambda i: (i, 0))] * 2,
        out_specs=[pl.BlockSpec((tokens, depth), lambda i: (0, i))]
        + [pl.BlockSpec((tokens, columns), lambda i: (0, 0))] * 2,
        out_shape=[jax.ShapeDtypeStruct((tokens, width), BF16)]
        + [jax.ShapeDtypeStruct((tokens, columns), F32)] * 2,
        compiler_params=params(40),
        cost_estimate=cost(4 * tokens * width * columns, 4 * width * columns),
    )(*pieces, w_gate, w_up)


def mid_kernel(count, width, per_expert, first_ref, *refs):
    pieces, refs = refs[:count], refs[count:]
    down_ref, a_ref, b_ref, c_ref, gg_ref, ug_ref, h_ref = refs
    step = pl.program_id(0)

    @pl.when(step == 0)
    def _():
        c_ref[...] = joined([p.at[:, :width] for p in pieces])

    gates = joined([p.at[:, width:] for p in pieces]).astype(F32)
    lane = lax.broadcasted_iota(jnp.int32, gates.shape, 1)
    own = first_ref[0] + step // per_expert
    weight = jnp.sum(jnp.where(lane == own, gates, 0.0), axis=1, keepdims=True)
    hidden_grad = weight * contract(c_ref[...], down_ref[...], 1, 1)
    a, b = a_ref[...], b_ref[...]
    g = jax.nn.sigmoid(a)
    active = a * g
    h_ref[...] = (weight * (active * b)).astype(BF16)
    ug_ref[...] = (hidden_grad * active).astype(BF16)
    gg_ref[...] = (hidden_grad * b * g * (1.0 + a * (1.0 - g))).astype(BF16)


def mid(first, pieces, w_down, a, b, experts):
    columns, width = w_down.shape
    tokens = a.shape[0]
    block = min(256, columns // experts)
    narrow = pl.BlockSpec((tokens, block), lambda i: (0, i))
    return pl.pallas_call(
        functools.partial(mid_kernel, len(pieces), width, columns // experts // block),
        grid=(columns // block,),
        in_specs=[pl.BlockSpec(memory_space=pltpu.SMEM)]
        + [pl.BlockSpec(p.shape, lambda i: (0, 0)) for p in pieces]
        + [pl.BlockSpec((block, width), lambda i: (i, 0)), narrow, narrow],
        out_specs=[pl.BlockSpec((tokens, width), lambda i: (0, 0))] + [narrow] * 3,
        out_shape=[jax.ShapeDtypeStruct((tokens, width), BF16)]
        + [jax.ShapeDtypeStruct((tokens, columns), BF16)] * 3,
        compiler_params=params(40),
        cost_estimate=cost(2 * tokens * width * columns, 2 * width * columns),
    )(first, *pieces, w_down, a, b)


def row_kernel(gg_ref, ug_ref, gate_ref, up_ref, far_ref, near_ref):
    rows = contract(gg_ref[...], gate_ref[...], 1, 1) + contract(ug_ref[...], up_ref[...], 1, 1)
    half = near_ref.shape[0]
    near_ref[...] = rows[:half].astype(BF16)
    far_ref[...] = rows[half:].astype(BF16)


def row(gg, ug, w_gate, w_up, part, parts):
    tokens, columns = gg.shape
    width = w_gate.shape[0] // parts
    block = min(512, width)
    base = part * (width // block)
    whole = pl.BlockSpec((tokens, columns), lambda i: (0, 0))
    return pl.pallas_call(
        row_kernel,
        grid=(width // block,),
        in_specs=[whole, whole] + [pl.BlockSpec((block, columns), lambda i: (base + i, 0))] * 2,
        out_specs=[pl.BlockSpec((tokens // 2, block), lambda i: (0, i))] * 2,
        out_shape=[jax.ShapeDtypeStruct((tokens // 2, width), BF16)] * 2,
        compiler_params=params(40),
        cost_estimate=cost(4 * tokens * width * columns, 4 * width * columns),
    )(gg, ug, w_gate, w_up)


def grads_kernel(x_ref, gg_ref, ug_ref, h_ref, c_ref, gate_ref, up_ref, down_ref):
    gate_ref[...] = contract(x_ref[...], gg_ref[...], 0, 0).astype(BF16)
    up_ref[...] = contract(x_ref[...], ug_ref[...], 0, 0).astype(BF16)
    down_ref[...] = contract(h_ref[...], c_ref[...], 0, 0).astype(BF16)


def grads(x, gg, ug, h, c):
    tokens, width = x.shape
    columns = gg.shape[1]
    steps = max(1, min(8, columns // LANES))
    high, low = width // steps, columns // steps
    tall = pl.BlockSpec((high, columns), lambda i: (i, 0))
    return pl.pallas_call(
        grads_kernel,
        grid=(steps,),
        in_specs=[
            pl.BlockSpec((tokens, high), lambda i: (0, i)),
            pl.BlockSpec((tokens, columns), lambda i: (0, 0)),
            pl.BlockSpec((tokens, columns), lambda i: (0, 0)),
            pl.BlockSpec((tokens, low), lambda i: (0, i)),
            pl.BlockSpec((tokens, width), lambda i: (0, 0)),
        ],
        out_specs=[tall, tall, pl.BlockSpec((low, width), lambda i: (i, 0))],
        out_shape=[jax.ShapeDtypeStruct((width, columns), BF16)] * 2
        + [jax.ShapeDtypeStruct((columns, width), BF16)],
        compiler_params=params(48),
        cost_estimate=cost(6 * tokens * width * columns, 6 * width * columns),
    )(x, gg, ug, h, c)


def deliver(near, far):
    devices, sections = lax.axis_size("expert"), lax.axis_size("section")
    mine = (near.astype(F32) + swap(far, 1).astype(F32)).astype(BF16)
    mine = mine.reshape(devices // 2, -1, near.shape[1])
    total = None
    for m in range(devices // 2):
        route = [
            (s * devices + i, (s - 1) % sections * devices + (i ^ (2 * m)))
            for s in range(sections)
            for i in range(devices)
        ]
        part = lax.ppermute(mine[m], ("section", "expert"), route).astype(F32)
        total = part if total is None else total + part
    return total.astype(BF16)


def body(layer_input, w_gate, w_up, w_down, grad_out, expert_ids, gates):
    devices = lax.axis_size("expert")
    experts = max(1, EXPERTS // devices)
    split = max(1, devices // EXPERTS)
    first = (lax.axis_index("expert") * experts // split).astype(jnp.int32).reshape(1)
    w_gate, w_up, w_down = w_gate[0], w_up[0], w_down[0]
    chosen = expert_ids[0][:, :, None] == lax.iota(jnp.int32, LANES)
    weight = jnp.sum(jnp.where(chosen, gates[0][:, :, None].astype(F32), 0.0), axis=1)
    message = jnp.concatenate([grad_out[0], weight.astype(BF16)], axis=1)
    inputs, cotangents = gather(layer_input[0]), gather(message)
    if devices > 8:
        inputs, cotangents = [jnp.concatenate(inputs)], [jnp.concatenate(cotangents)]
    x, a, b = pre(inputs, w_gate, w_up)
    c, gg, ug, h = mid(first, cotangents, w_down, a, b, experts)
    parts = 2
    rows = [row(gg, ug, w_gate, w_up, part, parts) for part in range(parts)]
    gate_grad, up_grad, down_grad = grads(x, gg, ug, h, c)
    grad_prev = jnp.concatenate([deliver(near, far) for far, near in rows], axis=1)
    return grad_prev[None], gate_grad[None], up_grad[None], down_grad[None]


def solution(mesh):
    tokens, columns = P("section", "expert", None), P("section", None, "expert")
    return jax.shard_map(
        body,
        mesh=mesh,
        in_specs=(tokens, columns, columns, tokens, tokens, tokens, tokens),
        out_specs=(tokens, columns, columns, tokens),
        check_vma=False,
    )
```

profile of v0, /device:TPU:0, one launch (start us, length us, event | category | flops | bytes accessed | tf_op | source)
XLA Modules:
  0.0 112.9 jit_solution(16702358845202053114)
XLA Ops:
  0.6 4.1 %collective-permute-start.8 = (bf16[16,4096]{1,0:T(8,128)(2,1)}, bf16[16,4096]{1,0:T(8,128)(2,1)S(1)}, u32[]{:S(2)}, u32[]{:S(2)}) collective-permute-start(bf16[16,4096]{1,0:T(8,128)(2,1)} %bitcast.15), channel_id=1, source_target_pairs={{0,4},{1,5},{2,6},{3,7},{4,0},{5,1},{6,2},{7,3},{8,12},{9,13},{10,... | collective-permute-start | bytes 393224 | tf_op jit(solution)/shard_map/ppermute | solution.py:24
  4.7 0.7 bitcast_convert_fusion
  5.4 0.1 copy.14
  5.5 0.8 copy.13
  6.2 0.1 select_reduce_fusion
  6.4 0.9 pad_maximum_fusion.refs_0_
  7.3 0.1 collective-permute-start.1
  7.4 1.9 %collective-permute-start.7 = (bf16[16,4096]{1,0:T(8,128)(2,1)}, bf16[16,4096]{1,0:T(8,128)(2,1)S(1)}, u32[]{:S(2)}, u32[]{:S(2)}) collective-permute-start(bf16[16,4096]{1,0:T(8,128)(2,1)} %bitcast.16), channel_id=1, source_target_pairs={{0,2},{1,3},{2,0},{3,1},{4,6},{5,7},{6,4},{7,5},{8,10},{9,11},{10,... | collective-permute-start | bytes 393224 | tf_op jit(solution)/shard_map/ppermute | solution.py:24
  9.3 0.0 collective-permute-start.10
  9.3 4.9 %collective-permute-done.8.refs_2_ = bf16[16,4096]{1,0:T(8,128)(2,1)S(1)} collective-permute-done((bf16[16,4096]{1,0:T(8,128)(2,1)}, bf16[16,4096]{1,0:T(8,128)(2,1)S(1)}, u32[]{:S(2)}, u32[]{:S(2)}) %collective-permute-start.8) | collective-permute-done | bytes 131104 | tf_op jit(solution)/shard_map/ppermute | solution.py:24
  14.2 0.9 collective-permute-start.9
  15.1 1.1 collective-permute-start
  16.2 0.9 collective-permute-done.1.refs_2_
  17.2 0.6 collective-permute-start.2
  17.8 0.0 collective-permute-done.7.refs_1_
  17.8 0.0 collective-permute-start.12
  17.8 0.0 collective-permute-done.10.refs_4_
  17.8 0.5 collective-permute-start.11
  18.3 2.3 %collective-permute-done.9.refs_3_ = bf16[16,4096]{1,0:T(8,128)(2,1)S(1)} collective-permute-done((bf16[16,4096]{1,0:T(8,128)(2,1)S(1)}, bf16[16,4096]{1,0:T(8,128)(2,1)S(1)}, u32[]{:S(2)}, u32[]{:S(2)}) %collective-permute-start.9) | collective-permute-done | bytes 131104 | tf_op jit(solution)/shard_map/ppermute | solution.py:24
  20.6 2.9 %collective-permute-done.refs_1_ = bf16[16,4224]{1,0:T(8,128)(2,1)S(1)} collective-permute-done((bf16[16,4224]{1,0:T(8,128)(2,1)S(1)}, bf16[16,4224]{1,0:T(8,128)(2,1)S(1)}, u32[]{:S(2)}, u32[]{:S(2)}) %collective-permute-start) | collective-permute-done | bytes 135200 | tf_op jit(solution)/shard_map/ppermute | solution.py:24
  23.5 0.0 collective-permute-start.3
  23.5 0.5 collective-permute-start.5
  24.1 0.1 collective-permute-start.4
  24.1 1.5 %collective-permute-done.2.refs_3_ = bf16[16,4224]{1,0:T(8,128)(2,1)S(1)} collective-permute-done((bf16[16,4224]{1,0:T(8,128)(2,1)S(1)}, bf16[16,4224]{1,0:T(8,128)(2,1)S(1)}, u32[]{:S(2)}, u32[]{:S(2)}) %collective-permute-start.2) | collective-permute-done | bytes 135200 | tf_op jit(solution)/shard_map/ppermute | solution.py:24
  25.7 0.0 collective-permute-start.6
  25.7 0.9 copy-done
  26.6 14.1 %shard_map.102 = (bf16[128,4096]{1,0:T(8,128)(2,1)S(1)}, f32[128,2048]{1,0:T(8,128)S(1)}, f32[128,2048]{1,0:T(8,128)S(1)}) custom-call(bf16[16,4096]{1,0:T(8,128)(2,1)S(1)} %bitcast.18, bf16[16,4096]{1,0:T(8,128)(2,1)S(1)} %collective-permute-done.7.refs_1_, bf16[16,4096]{1,0:T(8,128)(2,1)S(1)} %collective-permute-done.8.refs_2_, ...), custom_call_target="tpu_custom_call" | custom-call | flops 4294967296 | bytes 33554432 | tf_op jit(solution)/shard_map/pallas_call | solution.py:73
  40.7 0.0 collective-permute-done.5.refs_6_
  40.7 0.0 collective-permute-done.4.refs_5_
  40.7 11.3 %shard_map.103 = (bf16[128,4096]{1,0:T(8,128)(2,1)S(1)}, bf16[128,2048]{1,0:T(8,128)(2,1)S(1)}, bf16[128,2048]{1,0:T(8,128)(2,1)S(1)}, bf16[128,2048]{1,0:T(8,128)(2,1)S(1)}) custom-call(s32[1]{0:T(128)} %bitcast.first_ref, bf16[16,4224]{1,0:T(8,128)(2,1)S(1)} %pad_maximum_fusion.refs_0_, bf16[16,4224]{1,0:T(8,128)(2,1)S(1)} %collective-permute-done.refs_1_, ...), custom_call_target="tpu_custom_call" | custom-call | flops 2147483648 | bytes 16777216 | tf_op jit(solution)/shard_map/pallas_call | solution.py:114
  52.0 9.2 %shard_map.104 = (bf16[64,2048]{1,0:T(8,128)(2,1)S(1)}, bf16[64,2048]{1,0:T(8,128)(2,1)S(1)}) custom-call(bf16[128,2048]{1,0:T(8,128)(2,1)S(1)} %get-tuple-element.20.gg_ref, bf16[128,2048]{1,0:T(8,128)(2,1)S(1)} %get-tuple-element.21.ug_ref, bf16[4096,2048]{1,0:T(8,128)(2,1)} %bitcast.20, bf16[4096,2048]{1,0:T(8,128)(2,1)} %bitcast.23), custom_call_target="tpu_custom_call" | custom-call | flops 2147483648 | bytes 16777216 | tf_op jit(solution)/shard_map/pallas_call | solution.py:141
  61.2 9.3 %shard_map.105 = (bf16[64,2048]{1,0:T(8,128)(2,1)S(1)}, bf16[64,2048]{1,0:T(8,128)(2,1)S(1)}) custom-call(bf16[128,2048]{1,0:T(8,128)(2,1)S(1)} %get-tuple-element.20.gg_ref, bf16[128,2048]{1,0:T(8,128)(2,1)S(1)} %get-tuple-element.21.ug_ref, bf16[4096,2048]{1,0:T(8,128)(2,1)} %bitcast.21, bf16[4096,2048]{1,0:T(8,128)(2,1)} %bitcast.24), custom_call_target="tpu_custom_call" | custom-call | flops 2147483648 | bytes 16777216 | tf_op jit(solution)/shard_map/pallas_call | solution.py:141
  70.5 0.6 collective-permute-start.14
  71.1 0.1 collective-permute-start.19
  71.2 17.5 %shard_map.106 = (bf16[4096,2048]{1,0:T(8,128)(2,1)}, bf16[4096,2048]{1,0:T(8,128)(2,1)}, bf16[2048,4096]{1,0:T(8,128)(2,1)}) custom-call(bf16[128,4096]{1,0:T(8,128)(2,1)S(1)} %get-tuple-element.26.x_ref, bf16[128,2048]{1,0:T(8,128)(2,1)S(1)} %get-tuple-element.20.gg_ref, bf16[128,2048]{1,0:T(8,128)(2,1)S(1)} %get-tuple-element.21.ug_ref, ...), custom_call_target="tpu_custom_call" | custom-call | flops 6442450944 | bytes 50331648 | tf_op jit(solution)/shard_map/pallas_call | solution.py:164
  88.7 0.0 collective-permute-done.14
  88.7 0.1 add_convert_fusion.1
  88.8 2.5 %collective-permute-start.15 = (bf16[16,2048]{1,0:T(8,128)(2,1)S(1)}, bf16[16,2048]{1,0:T(8,128)(2,1)S(1)}, u32[]{:S(2)}, u32[]{:S(2)}) collective-permute-start(bf16[16,2048]{1,0:T(8,128)(2,1)S(1)} %get-tuple-element.32), channel_id=1, source_target_pairs={{0,24},{1,25},{2,26},{3,27},{4,28},{5,29},{6,30},{7,31},{8,0},{9,1... | collective-permute-start | bytes 196616 | tf_op jit(solution)/shard_map/ppermute | solution.py:193
  91.4 0.5 collective-permute-start.16
  91.8 5.6 %collective-permute-start.17 = (bf16[16,2048]{1,0:T(8,128)(2,1)S(1)}, bf16[16,2048]{1,0:T(8,128)(2,1)S(1)}, u32[]{:S(2)}, u32[]{:S(2)}) collective-permute-start(bf16[16,2048]{1,0:T(8,128)(2,1)S(1)} %get-tuple-element.34), channel_id=1, source_target_pairs={{0,28},{1,29},{2,30},{3,31},{4,24},{5,25},{6,26},{7,27},{8,4},{9,5... | collective-permute-start | bytes 196616 | tf_op jit(solution)/shard_map/ppermute | solution.py:193
  97.4 0.1 add_convert_fusion
  97.5 1.6 %collective-permute-start.20 = (bf16[16,2048]{1,0:T(8,128)(2,1)S(1)}, bf16[16,2048]{1,0:T(8,128)(2,1)S(1)}, u32[]{:S(2)}, u32[]{:S(2)}) collective-permute-start(bf16[16,2048]{1,0:T(8,128)(2,1)S(1)} %get-tuple-element.36), channel_id=1, source_target_pairs={{0,24},{1,25},{2,26},{3,27},{4,28},{5,29},{6,30},{7,31},{8,0},{9,1... | collective-permute-start | bytes 196616 | tf_op jit(solution)/shard_map/ppermute | solution.py:193
  99.2 1.4 %collective-permute-start.21 = (bf16[16,2048]{1,0:T(8,128)(2,1)S(1)}, bf16[16,2048]{1,0:T(8,128)(2,1)S(1)}, u32[]{:S(2)}, u32[]{:S(2)}) collective-permute-start(bf16[16,2048]{1,0:T(8,128)(2,1)S(1)} %get-tuple-element.39), channel_id=1, source_target_pairs={{0,26},{1,27},{2,24},{3,25},{4,30},{5,31},{6,28},{7,29},{8,2},{9,3... | collective-permute-start | bytes 196616 | tf_op jit(solution)/shard_map/ppermute | solution.py:193
  100.6 4.7 %collective-permute-start.22 = (bf16[16,2048]{1,0:T(8,128)(2,1)S(1)}, bf16[16,2048]{1,0:T(8,128)(2,1)S(1)}, u32[]{:S(2)}, u32[]{:S(2)}) collective-permute-start(bf16[16,2048]{1,0:T(8,128)(2,1)S(1)} %get-tuple-element.38), channel_id=1, source_target_pairs={{0,28},{1,29},{2,30},{3,31},{4,24},{5,25},{6,26},{7,27},{8,4},{9,5... | collective-permute-start | bytes 196616 | tf_op jit(solution)/shard_map/ppermute | solution.py:193
  105.2 1.6 %collective-permute-start.23 = (bf16[16,2048]{1,0:T(8,128)(2,1)S(1)}, bf16[16,2048]{1,0:T(8,128)(2,1)S(1)}, u32[]{:S(2)}, u32[]{:S(2)}) collective-permute-start(bf16[16,2048]{1,0:T(8,128)(2,1)S(1)} %get-tuple-element.37), channel_id=1, source_target_pairs={{0,30},{1,31},{2,28},{3,29},{4,26},{5,27},{6,24},{7,25},{8,6},{9,7... | collective-permute-start | bytes 196616 | tf_op jit(solution)/shard_map/ppermute | solution.py:193
  106.9 1.5 %collective-permute-done.22 = bf16[16,2048]{1,0:T(8,128)(2,1)S(1)} collective-permute-done((bf16[16,2048]{1,0:T(8,128)(2,1)S(1)}, bf16[16,2048]{1,0:T(8,128)(2,1)S(1)}, u32[]{:S(2)}, u32[]{:S(2)}) %collective-permute-start.22) | collective-permute-done | bytes 65568 | tf_op jit(solution)/shard_map/ppermute | solution.py:193
  108.4 3.8 %collective-permute-done.23 = bf16[16,2048]{1,0:T(8,128)(2,1)S(1)} collective-permute-done((bf16[16,2048]{1,0:T(8,128)(2,1)S(1)}, bf16[16,2048]{1,0:T(8,128)(2,1)S(1)}, u32[]{:S(2)}, u32[]{:S(2)}) %collective-permute-start.23) | collective-permute-done | bytes 65568 | tf_op jit(solution)/shard_map/ppermute | solution.py:193
  112.3 0.7 maximum_bitcast_fusion
  (19 shorter events, 0.2 us)
Async XLA Ops:
  0.6 13.6 %collective-permute-start.8 = (bf16[16,4096]{1,0:T(8,128)(2,1)}, bf16[16,4096]{1,0:T(8,128)(2,1)S(1)}, u32[]{:S(2)}, u32[]{:S(2)}) collective-permute-start(bf16[16,4096]{1,0:T(8,128)(2,1)} %bitcast.15), channel_id=1, source_target_pairs={{0,4},{1,5},{2,6},{3,7},{4,0},{5,1},{6,2},{7,3},{8,12},{9,13},{10,... | collective-permute-start | bytes 393224 | tf_op jit(solution)/shard_map/ppermute | solution.py:24
  7.3 9.9 %collective-permute-start.1 = (bf16[16,4224]{1,0:T(8,128)(2,1)S(1)}, bf16[16,4224]{1,0:T(8,128)(2,1)S(1)}, u32[]{:S(2)}, u32[]{:S(2)}) collective-permute-start(bf16[16,4224]{1,0:T(8,128)(2,1)S(1)} %pad_maximum_fusion.refs_0_), channel_id=1, source_target_pairs={{0,4},{1,5},{2,6},{3,7},{4,0},{5,1},{6,2},{7,3},{8,12},{9,13},{10,... | collective-permute-start | bytes 405512 | tf_op jit(solution)/shard_map/ppermute | solution.py:24
  7.4 10.4 %collective-permute-start.7 = (bf16[16,4096]{1,0:T(8,128)(2,1)}, bf16[16,4096]{1,0:T(8,128)(2,1)S(1)}, u32[]{:S(2)}, u32[]{:S(2)}) collective-permute-start(bf16[16,4096]{1,0:T(8,128)(2,1)} %bitcast.16), channel_id=1, source_target_pairs={{0,2},{1,3},{2,0},{3,1},{4,6},{5,7},{6,4},{7,5},{8,10},{9,11},{10,... | collective-permute-start | bytes 393224 | tf_op jit(solution)/shard_map/ppermute | solution.py:24
  9.3 8.6 %collective-permute-start.10 = (bf16[16,4096]{1,0:T(8,128)(2,1)}, bf16[16,4096]{1,0:T(8,128)(2,1)S(1)}, u32[]{:S(2)}, u32[]{:S(2)}) collective-permute-start(bf16[16,4096]{1,0:T(8,128)(2,1)} %bitcast.17), channel_id=1, source_target_pairs={{0,1},{1,0},{2,3},{3,2},{4,5},{5,4},{6,7},{7,6},{8,9},{9,8},{10,11... | collective-permute-start | bytes 393224 | tf_op jit(solution)/shard_map/ppermute | solution.py:24
  14.2 6.4 %collective-permute-start.9 = (bf16[16,4096]{1,0:T(8,128)(2,1)S(1)}, bf16[16,4096]{1,0:T(8,128)(2,1)S(1)}, u32[]{:S(2)}, u32[]{:S(2)}) collective-permute-start(bf16[16,4096]{1,0:T(8,128)(2,1)S(1)} %collective-permute-done.8.refs_2_), channel_id=1, source_target_pairs={{0,2},{1,3},{2,0},{3,1},{4,6},{5,7},{6,4},{7,5},{8,10},{9,11},{10,... | collective-permute-start | bytes 393224 | tf_op jit(solution)/shard_map/ppermute | solution.py:24
  15.1 8.4 %collective-permute-start = (bf16[16,4224]{1,0:T(8,128)(2,1)S(1)}, bf16[16,4224]{1,0:T(8,128)(2,1)S(1)}, u32[]{:S(2)}, u32[]{:S(2)}) collective-permute-start(bf16[16,4224]{1,0:T(8,128)(2,1)S(1)} %pad_maximum_fusion.refs_0_), channel_id=1, source_target_pairs={{0,2},{1,3},{2,0},{3,1},{4,6},{5,7},{6,4},{7,5},{8,10},{9,11},{10,... | collective-permute-start | bytes 405512 | tf_op jit(solution)/shard_map/ppermute | solution.py:24
  17.2 8.5 %collective-permute-start.2 = (bf16[16,4224]{1,0:T(8,128)(2,1)S(1)}, bf16[16,4224]{1,0:T(8,128)(2,1)S(1)}, u32[]{:S(2)}, u32[]{:S(2)}) collective-permute-start(bf16[16,4224]{1,0:T(8,128)(2,1)S(1)} %collective-permute-done.1.refs_2_), channel_id=1, source_target_pairs={{0,2},{1,3},{2,0},{3,1},{4,6},{5,7},{6,4},{7,5},{8,10},{9,11},{10,... | collective-permute-start | bytes 405512 | tf_op jit(solution)/shard_map/ppermute | solution.py:24
  17.8 5.7 %collective-permute-start.12 = (bf16[16,4096]{1,0:T(8,128)(2,1)S(1)}, bf16[16,4096]{1,0:T(8,128)(2,1)S(1)}, u32[]{:S(2)}, u32[]{:S(2)}) collective-permute-start(bf16[16,4096]{1,0:T(8,128)(2,1)S(1)} %collective-permute-done.8.refs_2_), channel_id=1, source_target_pairs={{0,1},{1,0},{2,3},{3,2},{4,5},{5,4},{6,7},{7,6},{8,9},{9,8},{10,11... | collective-permute-start | bytes 393224 | tf_op jit(solution)/shard_map/ppermute | solution.py:24
  17.8 6.2 %collective-permute-start.11 = (bf16[16,4096]{1,0:T(8,128)(2,1)S(1)}, bf16[16,4096]{1,0:T(8,128)(2,1)S(1)}, u32[]{:S(2)}, u32[]{:S(2)}) collective-permute-start(bf16[16,4096]{1,0:T(8,128)(2,1)S(1)} %collective-permute-done.7.refs_1_), channel_id=1, source_target_pairs={{0,1},{1,0},{2,3},{3,2},{4,5},{5,4},{6,7},{7,6},{8,9},{9,8},{10,11... | collective-permute-start | bytes 393224 | tf_op jit(solution)/shard_map/ppermute | solution.py:24
  20.6 5.0 %collective-permute-start.13 = (bf16[16,4096]{1,0:T(8,128)(2,1)S(1)}, bf16[16,4096]{1,0:T(8,128)(2,1)S(1)}, u32[]{:S(2)}, u32[]{:S(2)}) collective-permute-start(bf16[16,4096]{1,0:T(8,128)(2,1)S(1)} %collective-permute-done.9.refs_3_), channel_id=1, source_target_pairs={{0,1},{1,0},{2,3},{3,2},{4,5},{5,4},{6,7},{7,6},{8,9},{9,8},{10,11... | collective-permute-start | bytes 393224 | tf_op jit(solution)/shard_map/ppermute | solution.py:24
  23.5 17.1 %collective-permute-start.3 = (bf16[16,4224]{1,0:T(8,128)(2,1)S(1)}, bf16[16,4224]{1,0:T(8,128)(2,1)S(1)}, u32[]{:S(2)}, u32[]{:S(2)}) collective-permute-start(bf16[16,4224]{1,0:T(8,128)(2,1)S(1)} %pad_maximum_fusion.refs_0_), channel_id=1, source_target_pairs={{0,1},{1,0},{2,3},{3,2},{4,5},{5,4},{6,7},{7,6},{8,9},{9,8},{10,11... | collective-permute-start | bytes 405512 | tf_op jit(solution)/shard_map/ppermute | solution.py:24
  23.5 17.1 %collective-permute-start.5 = (bf16[16,4224]{1,0:T(8,128)(2,1)S(1)}, bf16[16,4224]{1,0:T(8,128)(2,1)S(1)}, u32[]{:S(2)}, u32[]{:S(2)}) collective-permute-start(bf16[16,4224]{1,0:T(8,128)(2,1)S(1)} %collective-permute-done.1.refs_2_), channel_id=1, source_target_pairs={{0,1},{1,0},{2,3},{3,2},{4,5},{5,4},{6,7},{7,6},{8,9},{9,8},{10,11... | collective-permute-start | bytes 405512 | tf_op jit(solution)/shard_map/ppermute | solution.py:24
  24.1 16.6 %collective-permute-start.4 = (bf16[16,4224]{1,0:T(8,128)(2,1)S(1)}, bf16[16,4224]{1,0:T(8,128)(2,1)S(1)}, u32[]{:S(2)}, u32[]{:S(2)}) collective-permute-start(bf16[16,4224]{1,0:T(8,128)(2,1)S(1)} %collective-permute-done.refs_1_), channel_id=1, source_target_pairs={{0,1},{1,0},{2,3},{3,2},{4,5},{5,4},{6,7},{7,6},{8,9},{9,8},{10,11... | collective-permute-start | bytes 405512 | tf_op jit(solution)/shard_map/ppermute | solution.py:24
  25.7 15.0 %collective-permute-start.6 = (bf16[16,4224]{1,0:T(8,128)(2,1)S(1)}, bf16[16,4224]{1,0:T(8,128)(2,1)S(1)}, u32[]{:S(2)}, u32[]{:S(2)}) collective-permute-start(bf16[16,4224]{1,0:T(8,128)(2,1)S(1)} %collective-permute-done.2.refs_3_), channel_id=1, source_target_pairs={{0,1},{1,0},{2,3},{3,2},{4,5},{5,4},{6,7},{7,6},{8,9},{9,8},{10,11... | collective-permute-start | bytes 405512 | tf_op jit(solution)/shard_map/ppermute | solution.py:24
  25.7 0.9 copy-start
  70.5 18.2 %collective-permute-start.14 = (bf16[64,2048]{1,0:T(8,128)(2,1)S(1)}, bf16[64,2048]{1,0:T(8,128)(2,1)S(1)}, u32[]{:S(2)}, u32[]{:S(2)}) collective-permute-start(bf16[64,2048]{1,0:T(8,128)(2,1)S(1)} %get-tuple-element.23), channel_id=1, source_target_pairs={{0,1},{1,0},{2,3},{3,2},{4,5},{5,4},{6,7},{7,6},{8,9},{9,8},{10,11... | collective-permute-start | bytes 786440 | tf_op jit(solution)/shard_map/ppermute | solution.py:24
  71.1 26.4 %collective-permute-start.19 = (bf16[64,2048]{1,0:T(8,128)(2,1)S(1)}, bf16[64,2048]{1,0:T(8,128)(2,1)S(1)}, u32[]{:S(2)}, u32[]{:S(2)}) collective-permute-start(bf16[64,2048]{1,0:T(8,128)(2,1)S(1)} %get-tuple-element.25), channel_id=1, source_target_pairs={{0,1},{1,0},{2,3},{3,2},{4,5},{5,4},{6,7},{7,6},{8,9},{9,8},{10,11... | collective-permute-start | bytes 786440 | tf_op jit(solution)/shard_map/ppermute | solution.py:24
  88.8 10.3 %collective-permute-start.15 = (bf16[16,2048]{1,0:T(8,128)(2,1)S(1)}, bf16[16,2048]{1,0:T(8,128)(2,1)S(1)}, u32[]{:S(2)}, u32[]{:S(2)}) collective-permute-start(bf16[16,2048]{1,0:T(8,128)(2,1)S(1)} %get-tuple-element.32), channel_id=1, source_target_pairs={{0,24},{1,25},{2,26},{3,27},{4,28},{5,29},{6,30},{7,31},{8,0},{9,1... | collective-permute-start | bytes 196616 | tf_op jit(solution)/shard_map/ppermute | solution.py:193
  91.4 9.2 %collective-permute-start.16 = (bf16[16,2048]{1,0:T(8,128)(2,1)S(1)}, bf16[16,2048]{1,0:T(8,128)(2,1)S(1)}, u32[]{:S(2)}, u32[]{:S(2)}) collective-permute-start(bf16[16,2048]{1,0:T(8,128)(2,1)S(1)} %get-tuple-element.35), channel_id=1, source_target_pairs={{0,26},{1,27},{2,24},{3,25},{4,30},{5,31},{6,28},{7,29},{8,2},{9,3... | collective-permute-start | bytes 196616 | tf_op jit(solution)/shard_map/ppermute | solution.py:193
  91.8 13.4 %collective-permute-start.17 = (bf16[16,2048]{1,0:T(8,128)(2,1)S(1)}, bf16[16,2048]{1,0:T(8,128)(2,1)S(1)}, u32[]{:S(2)}, u32[]{:S(2)}) collective-permute-start(bf16[16,2048]{1,0:T(8,128)(2,1)S(1)} %get-tuple-element.34), channel_id=1, source_target_pairs={{0,28},{1,29},{2,30},{3,31},{4,24},{5,25},{6,26},{7,27},{8,4},{9,5... | collective-permute-start | bytes 196616 | tf_op jit(solution)/shard_map/ppermute | solution.py:193
  97.4 9.4 %collective-permute-start.18 = (bf16[16,2048]{1,0:T(8,128)(2,1)S(1)}, bf16[16,2048]{1,0:T(8,128)(2,1)S(1)}, u32[]{:S(2)}, u32[]{:S(2)}) collective-permute-start(bf16[16,2048]{1,0:T(8,128)(2,1)S(1)} %get-tuple-element.33), channel_id=1, source_target_pairs={{0,30},{1,31},{2,28},{3,29},{4,26},{5,27},{6,24},{7,25},{8,6},{9,7... | collective-permute-start | bytes 196616 | tf_op jit(solution)/shard_map/ppermute | solution.py:193
  97.5 9.3 %collective-permute-start.20 = (bf16[16,2048]{1,0:T(8,128)(2,1)S(1)}, bf16[16,2048]{1,0:T(8,128)(2,1)S(1)}, u32[]{:S(2)}, u32[]{:S(2)}) collective-permute-start(bf16[16,2048]{1,0:T(8,128)(2,1)S(1)} %get-tuple-element.36), channel_id=1, source_target_pairs={{0,24},{1,25},{2,26},{3,27},{4,28},{5,29},{6,30},{7,31},{8,0},{9,1... | collective-permute-start | bytes 196616 | tf_op jit(solution)/shard_map/ppermute | solution.py:193
  99.2 7.7 %collective-permute-start.21 = (bf16[16,2048]{1,0:T(8,128)(2,1)S(1)}, bf16[16,2048]{1,0:T(8,128)(2,1)S(1)}, u32[]{:S(2)}, u32[]{:S(2)}) collective-permute-start(bf16[16,2048]{1,0:T(8,128)(2,1)S(1)} %get-tuple-element.39), channel_id=1, source_target_pairs={{0,26},{1,27},{2,24},{3,25},{4,30},{5,31},{6,28},{7,29},{8,2},{9,3... | collective-permute-start | bytes 196616 | tf_op jit(solution)/shard_map/ppermute | solution.py:193
  100.6 7.9 %collective-permute-start.22 = (bf16[16,2048]{1,0:T(8,128)(2,1)S(1)}, bf16[16,2048]{1,0:T(8,128)(2,1)S(1)}, u32[]{:S(2)}, u32[]{:S(2)}) collective-permute-start(bf16[16,2048]{1,0:T(8,128)(2,1)S(1)} %get-tuple-element.38), channel_id=1, source_target_pairs={{0,28},{1,29},{2,30},{3,31},{4,24},{5,25},{6,26},{7,27},{8,4},{9,5... | collective-permute-start | bytes 196616 | tf_op jit(solution)/shard_map/ppermute | solution.py:193
  105.2 7.0 %collective-permute-start.23 = (bf16[16,2048]{1,0:T(8,128)(2,1)S(1)}, bf16[16,2048]{1,0:T(8,128)(2,1)S(1)}, u32[]{:S(2)}, u32[]{:S(2)}) collective-permute-start(bf16[16,2048]{1,0:T(8,128)(2,1)S(1)} %get-tuple-element.37), channel_id=1, source_target_pairs={{0,30},{1,31},{2,28},{3,29},{4,26},{5,27},{6,24},{7,25},{8,6},{9,7... | collective-permute-start | bytes 196616 | tf_op jit(solution)/shard_map/ppermute | solution.py:193
where the time goes:
time: 113 us
  Pallas kernels  61.4 us (54%)
  starting transfers between devices  28.4 us (25%)
  waiting for transfers between devices  18 us (16%)
  other arithmetic  2.58 us (2%)
  local copies, waits for them, and re-layouts  1.77 us (2%)
    pallas_call x2, Pallas kernels, row(): pl.pallas_call(row_kernel, grid=(width // block,), in_specs=[whole, whole...  18.5 us
    ppermute x8, starting transfers between devices, deliver(): part = lax.ppermute(mine[m], ('section', 'expert'), route).astype(F32)  17.9 us
    pallas_call x1, Pallas kernels, grads(): pl.pallas_call(grads_kernel, grid=(steps,), in_specs=[pl.BlockSpec((token...  17.5 us
    pallas_call x1, Pallas kernels, pre(): pl.pallas_call(functools.partial(pre_kernel, len(pieces)), grid=(width //...  14.1 us
    ppermute x16, waiting for transfers between devices, swap(): lax.ppermute(block, 'expert', [(i, i ^ bits) for i in range(devices)])  12.6 us
    pallas_call x1, Pallas kernels, mid(): pl.pallas_call(functools.partial(mid_kernel, len(pieces), width, columns...  11.3 us
    ppermute x16, starting transfers between devices, swap(): lax.ppermute(block, 'expert', [(i, i ^ bits) for i in range(devices)])  10.5 us
    ppermute x8, waiting for transfers between devices, deliver(): part = lax.ppermute(mine[m], ('section', 'expert'), route).astype(F32)  5.33 us
  transfers between devices with their start and end apart: 24, of which 7 were waited for; matrix products, arithmetic and copies ran while one was open for 2% of the time, Pallas kernels for 28%

commit v1 on v0

v1 whole, which is shorter than its diff:
```python
import functools

import jax
import jax.numpy as jnp
from jax import lax
from jax.experimental import pallas as pl
from jax.experimental.pallas import tpu as pltpu
from jax.sharding import PartitionSpec as P

EXPERTS = 16
LANES = 128
SLOTS = 5
BF16, F32 = jnp.bfloat16, jnp.float32
MIB = 1 << 20
WHOLE = pl.BlockSpec(memory_space=pltpu.VMEM)


def contract(left, right, left_dim, right_dim):
    return lax.dot_general(
        left, right, (((left_dim,), (right_dim,)), ((), ())), preferred_element_type=F32
    )


def swap(block, bits):
    devices = lax.axis_size("expert")
    return lax.ppermute(block, "expert", [(i, i ^ bits) for i in range(devices)])


def across(block, token):
    devices = lax.axis_size("expert")
    found = {0: block}
    bits = devices // 2
    while bits > 1:
        found |= {mask | bits: swap(part, bits) for mask, part in found.items()}
        if token is not None and bits == devices // 2:
            found[bits], token = lax.optimization_barrier((found[bits], token))
        bits //= 2
    return found, token


def gather(block, token=None):
    near, token = across(block, token)
    masks = sorted(near)
    return [near[m] for m in masks] + [swap(near[m], 1) for m in masks], token


def in_hbm(array):
    return pltpu.with_memory_space_constraint(array, pltpu.HBM)


def kernel_call(kernel, operands, outs, limit, flops, moved, **more):
    specs = more.pop("in_specs", [WHOLE] * len(operands))
    return pl.pallas_call(
        kernel,
        in_specs=specs,
        out_specs=more.pop("out_specs", [WHOLE] * len(outs)),
        out_shape=outs,
        compiler_params=pltpu.CompilerParams(vmem_limit_bytes=limit * MIB),
        cost_estimate=pl.CostEstimate(flops=flops, bytes_accessed=moved, transcendentals=0),
        **more,
    )(*operands)


def joined(refs, columns):
    parts = [r[:, columns] for r in refs]
    return jnp.concatenate(parts, axis=0) if len(parts) > 1 else parts[0]


def fetch_kernel(pieces, from_ref, to_ref, token_ref, sems):
    token_ref[...] = jnp.zeros_like(token_ref)
    rows = from_ref.shape[0] // pieces
    parts = [pl.ds(i * rows, rows) for i in range(pieces)]
    copies = [
        pltpu.make_async_copy(from_ref.at[part], to_ref.at[part], sems.at[i])
        for i, part in enumerate(parts)
    ]
    for copy in copies:
        copy.start()
    for copy in copies:
        copy.wait()


def fetch(weights, pieces=4):
    return kernel_call(
        functools.partial(fetch_kernel, pieces),
        [in_hbm(weights)],
        [pltpu.VMEM(weights.shape, weights.dtype), jax.ShapeDtypeStruct((8, LANES), F32)],
        1,
        0,
        2 * weights.size,
        in_specs=[pl.BlockSpec(memory_space=pltpu.HBM)],
        scratch_shapes=[pltpu.SemaphoreType.DMA((pieces,))],
    )


def pre_kernel(count, *refs):
    pieces, refs = refs[:count], refs[count + 1 :]
    gate_ref, up_ref, at_ref, bt_ref, xt_ref, a_ref, b_ref = refs
    width = gate_ref.shape[0]
    depth = min(512, width)
    for start in range(0, width, depth):
        rows = pl.ds(start, depth)
        x = joined(pieces, rows)
        xt_ref[rows, :] = x.T
        a = jnp.dot(x, gate_ref[rows, :], preferred_element_type=F32)
        b = jnp.dot(x, up_ref[rows, :], preferred_element_type=F32)
        if start:
            a, b = a_ref[...] + a, b_ref[...] + b
        a_ref[...], b_ref[...] = a, b
    at_ref[...], bt_ref[...] = a_ref[...].T, b_ref[...].T


def pre(pieces, token, w_gate, w_up):
    width, columns = w_gate.shape
    tokens = sum(p.shape[0] for p in pieces)
    count = len(pieces)
    return kernel_call(
        functools.partial(pre_kernel, count),
        [*pieces, token, w_gate, w_up],
        [jax.ShapeDtypeStruct((columns, tokens), F32)] * 2
        + [jax.ShapeDtypeStruct((width, tokens), BF16)],
        6,
        4 * tokens * width * columns,
        2 * tokens * width,
        scratch_shapes=[pltpu.VMEM((tokens, columns), F32)] * 2,
    )


def core_kernel(count, experts, split, *refs):
    pieces, refs = refs[:count], refs[count:]
    at_ref, bt_ref, down_ref, gate_ref, up_ref = refs[:5]
    c_ref, ggt_ref, ugt_ref, ht_ref, near_ref, far_ref = refs[5:11]
    downs, gate_slots, up_slots, down_sems, gate_sems, up_sems = refs[11:]
    columns, width = down_ref.shape
    each, block, depth = columns // experts, downs.shape[1], gate_slots.shape[1]
    steps, turns, half = columns // block, width // depth, near_ref.shape[0]
    ahead = SLOTS - 1

    def arrivals(ref, slots, sems, step):
        rows = pl.ds(pl.multiple_of(step * slots.shape[1], slots.shape[1]), slots.shape[1])
        slot = lax.rem(step, SLOTS)
        return pltpu.make_async_copy(ref.at[rows], slots.at[slot], sems.at[slot])

    def down(step):
        return arrivals(down_ref, downs, down_sems, step)

    def gate(turn):
        return arrivals(gate_ref, gate_slots, gate_sems, turn)

    def up(turn):
        return arrivals(up_ref, up_slots, up_sems, turn)

    def start_pair(turn):
        gate(turn).start()
        up(turn).start()

    for step in range(min(ahead, steps)):
        down(jnp.int32(step)).start()
    for turn in range(min(ahead, turns) - min(ahead, steps)):
        start_pair(jnp.int32(turn))
    at = 0
    for piece in pieces:
        c_ref[pl.ds(at, piece.shape[0]), :] = piece[:, :width]
        at += piece.shape[0]
    gates = joined(pieces, slice(width, None)).astype(F32).T
    line = lax.broadcasted_iota(jnp.int32, gates.shape, 0)
    first = lax.axis_index("expert") * experts // split
    begun = max(0, min(ahead, turns) - min(ahead, steps))

    def units(step, carry):
        down(step).wait()
        last = step + ahead - steps

        @pl.when(last < 0)
        def _():
            down(step + ahead).start()

        @pl.when((last >= begun) & (last < min(ahead, turns)))
        def _():
            start_pair(last)

        rows = pl.ds(pl.multiple_of(step * block, block), block)
        own = line == first + step * block // each
        weight = jnp.sum(jnp.where(own, gates, 0.0), axis=0, keepdims=True)
        hidden_grad = weight * contract(downs[lax.rem(step, SLOTS)], c_ref[...], 1, 1)
        a, b = at_ref[rows, :], bt_ref[rows, :]
        g = jax.nn.sigmoid(a)
        active = a * g
        ht_ref[rows, :] = (weight * (active * b)).astype(BF16)
        ugt_ref[rows, :] = (hidden_grad * active).astype(BF16)
        ggt_ref[rows, :] = (hidden_grad * b * g * (1.0 + a * (1.0 - g))).astype(BF16)
        return carry

    def rows_out(turn, carry):
        gate(turn).wait()
        up(turn).wait()

        @pl.when(turn + ahead < turns)
        def _():
            start_pair(turn + ahead)

        rows, slot = pl.ds(pl.multiple_of(turn * depth, depth), depth), lax.rem(turn, SLOTS)
        total = jnp.dot(gate_slots[slot], ggt_ref[...], preferred_element_type=F32)
        total += jnp.dot(up_slots[slot], ugt_ref[...], preferred_element_type=F32)
        total = total.T.astype(BF16)
        near_ref[:, rows] = total[:half]
        far_ref[:, rows] = total[half:]
        return carry

    lax.fori_loop(0, steps, units, 0)
    lax.fori_loop(0, turns, rows_out, 0)


def core(pieces, at, bt, w_down, w_gate, w_up, experts, split):
    columns, width = w_down.shape
    tokens = at.shape[1]
    block, depth = min(256, columns // experts), min(512, width)
    return kernel_call(
        functools.partial(core_kernel, len(pieces), experts, split),
        [*pieces, at, bt, in_hbm(w_down), in_hbm(w_gate), in_hbm(w_up)],
        [jax.ShapeDtypeStruct((tokens, width), BF16)]
        + [jax.ShapeDtypeStruct((columns, tokens), BF16)] * 3
        + [jax.ShapeDtypeStruct((tokens // 2, width), BF16)] * 2,
        40,
        12 * tokens * width * columns,
        6 * width * columns,
        in_specs=[WHOLE] * (len(pieces) + 2) + [pl.BlockSpec(memory_space=pltpu.HBM)] * 3,
        scratch_shapes=[pltpu.VMEM((SLOTS, block, width), BF16)]
        + [pltpu.VMEM((SLOTS, depth, columns), BF16)] * 2
        + [pltpu.SemaphoreType.DMA((SLOTS,))] * 3,
    )


def grads_kernel(form, *refs):
    count = len(form)
    operands, outs = refs[: 2 * count], refs[2 * count + 1 : 3 * count + 1]
    token_ref, slots, sems = refs[3 * count + 1 :]
    token_ref[...] = refs[2 * count][...]
    flying, turn = {}, 0
    for k, right_dim in enumerate(form):
        left, right, out = operands[2 * k], operands[2 * k + 1], outs[k]
        rows, columns = out.shape
        wide = slots.shape[2]
        block = slots.shape[1] * wide // columns
        for start in range(0, rows, slots.shape[1]):
            at = pl.ds(start, slots.shape[1])
            for side in range(0, columns, wide):
                slot = turn % SLOTS
                turn += 1
                if slot in flying:
                    flying.pop(slot).wait()
                part = pl.ds(side, wide)
                rhs = right[:, part] if right_dim == 0 else right[part, :]
                slots[slot] = contract(left[at, :], rhs, 1, right_dim).astype(BF16)
                flying[slot] = pltpu.make_async_copy(slots.at[slot], out.at[at, part], sems.at[slot])
                flying[slot].start()
    for copy in flying.values():
        copy.wait()


def grads(token, *products):
    operands, outs, form, flops = [], [], [], 0
    for left, right, right_dim in products:
        operands += [left, right]
        form.append(right_dim)
        outs.append(jax.ShapeDtypeStruct((left.shape[0], right.shape[1 - right_dim]), BF16))
        flops += 4 * left.size * right.shape[1 - right_dim]
    wide = min(2048, min(o.shape[1] for o in outs))
    high = min(512, min(o.shape[0] for o in outs))
    moved = sum(2 * o.size for o in outs)
    return kernel_call(
        functools.partial(grads_kernel, tuple(form)),
        [*operands, token],
        [*outs, jax.ShapeDtypeStruct(token.shape, token.dtype)],
        20,
        flops,
        moved,
        out_specs=[pl.BlockSpec(memory_space=pltpu.HBM)] * len(outs) + [WHOLE],
        scratch_shapes=[pltpu.VMEM((SLOTS, high, wide), BF16), pltpu.SemaphoreType.DMA((SLOTS,))],
    )


def hand_on(mine, mask):
    devices, sections = lax.axis_size("expert"), lax.axis_size("section")
    route = [
        (s * devices + i, (s - 1) % sections * devices + (i ^ (2 * mask)))
        for s in range(sections)
        for i in range(devices)
    ]
    return lax.ppermute(mine, ("section", "expert"), route)


def body(layer_input, w_gate, w_up, w_down, grad_out, expert_ids, gates):
    devices = lax.axis_size("expert")
    experts = max(1, EXPERTS // devices)
    split = max(1, devices // EXPERTS)
    w_gate, w_up, w_down = w_gate[0], w_up[0], w_down[0]
    chosen = expert_ids[0][:, :, None] == lax.iota(jnp.int32, LANES)
    weight = jnp.sum(jnp.where(chosen, gates[0][:, :, None].astype(F32), 0.0), axis=1)
    message = jnp.concatenate([grad_out[0], weight.astype(BF16)], axis=1)
    (gate_near, token), (up_near, _) = fetch(w_gate), fetch(w_up)
    inputs, token = gather(layer_input[0], token)
    cotangents, _ = gather(message)
    if devices > 8:
        inputs, cotangents = [jnp.concatenate(inputs)], [jnp.concatenate(cotangents)]
    at, bt, xt = pre(inputs, token, gate_near, up_near)
    c, ggt, ugt, ht, near, far = core(cotangents, at, bt, w_down, w_gate, w_up, experts, split)
    gate_grad, token = grads(token, (xt, ggt, 1))
    mine = (near.astype(F32) + swap(far, 1).astype(F32)).astype(BF16)
    chips = devices // 2
    mine = jnp.split(mine, chips)
    far_first = sorted(range(chips), reverse=True)
    early = [m for m in far_first if m >= chips - chips // 4 or m < chips // 4]
    late = [m for m in far_first if m not in early]
    mine, token = lax.optimization_barrier((mine, token))
    arrived = [hand_on(mine[m], m) for m in early]
    up_grad, token = grads(token, (xt, ugt, 1))
    mine, token = lax.optimization_barrier((mine, token))
    arrived += [hand_on(mine[m], m) for m in late]
    down_grad, _ = grads(token, (ht, c, 0))
    grad_prev = functools.reduce(jnp.add, [part.astype(F32) for part in arrived]).astype(BF16)
    return grad_prev[None], gate_grad[None], up_grad[None], down_grad[None]


def solution(mesh):
    tokens, columns = P("section", "expert", None), P("section", None, "expert")
    return jax.shard_map(
        body,
        mesh=mesh,
        in_specs=(tokens, columns, columns, tokens, tokens, tokens, tokens),
        out_specs=(tokens, columns, columns, tokens),
        check_vma=False,
    )
```

time: 113 us -> 83 us (0.73)
  waiting for transfers between devices: 18 us -> 3.32 us
  starting transfers between devices: 28.4 us -> 19.5 us
  Pallas kernels: 61.4 us -> 55.8 us
    ppermute x16 -> x15, waiting for transfers between devices: 12.6 us -> 3.31 us  [swap(): lax.ppermute(block, 'expert', [(i, i ^ bits) for i in range(devices)])]
    ppermute x8 -> x4, starting transfers between devices: 17.9 us -> 8.61 us  [hand_on(): return lax.ppermute(mine, ('section', 'expert'), route)]
    pallas_call x5 -> x7, Pallas kernels: 61.4 us -> 55.8 us  [kernel_call(): pl.pallas_call(kernel, in_specs=specs, out_specs=more.pop('out_specs', [W...]
    ppermute x8 -> x4, waiting for transfers between devices: 5.33 us -> 0.01 us  [hand_on(): return lax.ppermute(mine, ('section', 'expert'), route)]
    ppermute x16 -> x15, starting transfers between devices: 10.5 us -> 10.8 us  [swap(): lax.ppermute(block, 'expert', [(i, i ^ bits) for i in range(devices)])]
  transfers between devices with their start and end apart: 24 -> 19, of which waited for: 7 -> 1; matrix products, arithmetic and copies ran while one was open for 2% -> 3% of each run, Pallas kernels for 28% -> 45%
where the time goes in v1:
time: 83 us; the launch traced here: 82.8 us
  Pallas kernels  55.8 us (67%)
  starting transfers between devices  19.5 us (23%)
  waiting for transfers between devices  3.32 us (4%)
  other arithmetic  2.57 us (3%)
  local copies, waits for them, and re-layouts  0.87 us (1%)
    pallas_call x7, Pallas kernels, kernel_call(): pl.pallas_call(kernel, in_specs=specs, out_specs=more.pop('out_specs', [W...  55.8 us
    ppermute x15, starting transfers between devices, swap(): lax.ppermute(block, 'expert', [(i, i ^ bits) for i in range(devices)])  10.8 us
    ppermute x4, starting transfers between devices, hand_on(): return lax.ppermute(mine, ('section', 'expert'), route)  8.61 us
    ppermute x15, waiting for transfers between devices, swap(): lax.ppermute(block, 'expert', [(i, i ^ bits) for i in range(devices)])  3.31 us
  transfers between devices with their start and end apart: 19, of which 1 were waited for; matrix products, arithmetic and copies ran while one was open for 3% of the time, Pallas kernels for 45%

profile of v1, /device:TPU:0, one launch (start us, length us, event | category | flops | bytes accessed | tf_op | source)
XLA Modules:
  0.0 82.8 jit_solution(15206910960873043673)
XLA Ops:
  0.6 4.1 %collective-permute-start.8 = (bf16[16,4096]{1,0:T(8,128)(2,1)}, bf16[16,4096]{1,0:T(8,128)(2,1)S(1)}, u32[]{:S(2)}, u32[]{:S(2)}) collective-permute-start(bf16[16,4096]{1,0:T(8,128)(2,1)} %bitcast.14), channel_id=1, source_target_pairs={{0,4},{1,5},{2,6},{3,7},{4,0},{5,1},{6,2},{7,3},{8,12},{9,13},{10,... | collective-permute-start | bytes 393224 | tf_op jit(solution)/shard_map/ppermute | solution.py:26
  4.7 0.7 bitcast_convert_fusion
  5.4 0.1 copy.14
  5.5 0.8 copy.13
  6.2 0.1 select_reduce_fusion
  6.4 0.9 %pad_maximum_fusion.refs_0_ = bf16[16,4224]{1,0:T(8,128)(2,1)S(1)} fusion(bf16[16,128]{1,0:T(8,128)(2,1)S(1)} %select_reduce_fusion, bf16[16,4096]{1,0:T(8,128)(2,1)} %bitcast.23), kind=kLoop, calls=%fused_computation.2 | loop fusion | flops 270336 | bytes 270336 | tf_op jit(solution)/shard_map/concatenate | solution.py:300
  7.3 0.1 collective-permute-start.1
  7.4 0.1 collective-permute-start.10
  7.4 1.8 %collective-permute-start.7 = (bf16[16,4096]{1,0:T(8,128)(2,1)}, bf16[16,4096]{1,0:T(8,128)(2,1)S(1)}, u32[]{:S(2)}, u32[]{:S(2)}) collective-permute-start(bf16[16,4096]{1,0:T(8,128)(2,1)} %bitcast.16), channel_id=1, source_target_pairs={{0,2},{1,3},{2,0},{3,1},{4,6},{5,7},{6,4},{7,5},{8,10},{9,11},{10,... | collective-permute-start | bytes 393224 | tf_op jit(solution)/shard_map/ppermute | solution.py:26
  9.3 5.9 %shard_map.102 = (bf16[4096,2048]{1,0:T(8,128)(2,1)S(1)}, f32[8,128]{1,0:T(8,128)S(1)}) custom-call(bf16[4096,2048]{1,0:T(8,128)(2,1)} %bitcast.18), custom_call_target="tpu_custom_call" | custom-call | bytes 16777216 | tf_op jit(solution)/shard_map/pallas_call | solution.py:53
  15.2 0.0 collective-permute-done.8.refs_2_
  15.2 0.3 collective-permute-start.9
  15.5 1.8 %collective-permute-start = (bf16[16,4224]{1,0:T(8,128)(2,1)S(1)}, bf16[16,4224]{1,0:T(8,128)(2,1)S(1)}, u32[]{:S(2)}, u32[]{:S(2)}) collective-permute-start(bf16[16,4224]{1,0:T(8,128)(2,1)S(1)} %pad_maximum_fusion.refs_0_), channel_id=1, source_target_pairs={{0,2},{1,3},{2,0},{3,1},{4,6},{5,7},{6,4},{7,5},{8,10},{9,11},{10,... | collective-permute-start | bytes 405512 | tf_op jit(solution)/shard_map/ppermute | solution.py:26
  17.3 0.0 collective-permute-done.1.refs_2_
  17.3 0.5 collective-permute-start.2
  17.8 0.0 collective-permute-done.7.refs_1_
  17.8 0.0 collective-permute-start.11
  17.8 0.0 collective-permute-done.10.refs_4_
  17.8 0.5 collective-permute-start.12
  18.3 3.3 %collective-permute-done.9.refs_3_ = bf16[16,4096]{1,0:T(8,128)(2,1)S(1)} collective-permute-done((bf16[16,4096]{1,0:T(8,128)(2,1)S(1)}, bf16[16,4096]{1,0:T(8,128)(2,1)S(1)}, u32[]{:S(2)}, u32[]{:S(2)}) %collective-permute-start.9) | collective-permute-done | bytes 131104 | tf_op jit(solution)/shard_map/ppermute | solution.py:26
  21.6 0.0 collective-permute-start.13
  21.6 6.5 %shard_map.103 = (bf16[4096,2048]{1,0:T(8,128)(2,1)S(1)}, f32[8,128]{1,0:T(8,128)}) custom-call(bf16[4096,2048]{1,0:T(8,128)(2,1)} %bitcast.20), custom_call_target="tpu_custom_call" | custom-call | bytes 16777216 | tf_op jit(solution)/shard_map/pallas_call | solution.py:53
  28.1 0.0 collective-permute-done.refs_1_
  28.1 0.6 collective-permute-start.3
  28.7 0.0 collective-permute-done.11.refs_5_
  28.7 0.1 collective-permute-start.5
  28.8 0.0 collective-permute-done.12.refs_6_
  28.8 0.4 collective-permute-start.4
  29.2 0.0 collective-permute-done.2.refs_3_
  29.2 0.1 collective-permute-start.6
  29.3 0.0 collective-permute-done.13.refs_7_
  29.3 4.6 %shard_map.104 = (f32[2048,128]{1,0:T(8,128)S(1)}, f32[2048,128]{1,0:T(8,128)S(1)}, bf16[4096,128]{1,0:T(8,128)(2,1)S(1)}) custom-call(bf16[16,4096]{1,0:T(8,128)(2,1)S(1)} %bitcast.17, bf16[16,4096]{1,0:T(8,128)(2,1)S(1)} %collective-permute-done.7.refs_1_, bf16[16,4096]{1,0:T(8,128)(2,1)S(1)} %collective-permute-done.8.refs_2_, ...), custom_call_target="tpu_custom_call" | custom-call | flops 4294967296 | bytes 1048576 | tf_op jit(solution)/shard_map/pallas_call | solution.py:53
  33.9 0.0 collective-permute-done.5.refs_6_
  33.9 0.0 collective-permute-done.4.refs_5_
  33.9 18.4 %shard_map.105 = (bf16[128,4096]{1,0:T(8,128)(2,1)S(1)}, bf16[2048,128]{1,0:T(8,128)(2,1)S(1)}, bf16[2048,128]{1,0:T(8,128)(2,1)S(1)}, bf16[2048,128]{1,0:T(8,12...) custom-call(bf16[16,4224]{1,0:T(8,128)(2,1)S(1)} %pad_maximum_fusion.refs_0_, ...), custom_call_target="tpu_custom_call" | custom-call | flops 12884901888 | bytes 50331648 | tf_op jit(solution)/shard_map/pallas_call | solution.py:53
  52.3 0.5 collective-permute-start.14
  52.8 6.6 %shard_map.106 = (bf16[4096,2048]{1,0:T(8,128)(2,1)}, f32[8,128]{1,0:T(8,128)S(1)}) custom-call(bf16[4096,128]{1,0:T(8,128)(2,1)S(1)} %get-tuple-element.40.refs_0_, bf16[2048,128]{1,0:T(8,128)(2,1)S(1)} %get-tuple-element.41.refs_1_, f32[8,128]{1,0:T(8,128)S(1)} %get-tuple-element.33.refs_8_.refs_2_), custom_call_target="tpu_custom_call" | custom-call | flops 4294967296 | bytes 16777216 | tf_op jit(solution)/shard_map/pallas_call | solution.py:53
  59.4 0.1 add_convert_fusion
  59.6 6.5 %collective-permute-start.15 = (bf16[16,4096]{1,0:T(8,128)(2,1)S(1)}, bf16[16,4096]{1,0:T(8,128)(2,1)S(1)}, u32[]{:S(2)}, u32[]{:S(2)}) collective-permute-start(bf16[16,4096]{1,0:T(8,128)(2,1)S(1)} %get-tuple-element.43), channel_id=1, source_target_pairs={{0,30},{1,31},{2,28},{3,29},{4,26},{5,27},{6,24},{7,25},{8,6},{9,7... | collective-permute-start | bytes 393224 | tf_op jit(solution)/shard_map/ppermute | solution.py:290
  66.1 0.5 collective-permute-start.16
  66.7 6.6 %shard_map.107 = (bf16[4096,2048]{1,0:T(8,128)(2,1)}, f32[8,128]{1,0:T(8,128)S(1)}) custom-call(bf16[4096,128]{1,0:T(8,128)(2,1)S(1)} %get-tuple-element.40.refs_0_, bf16[2048,128]{1,0:T(8,128)(2,1)S(1)} %get-tuple-element.47.refs_1_, f32[8,128]{1,0:T(8,128)S(1)} %get-tuple-element.48.refs_2_), custom_call_target="tpu_custom_call" | custom-call | flops 4294967296 | bytes 16777216 | tf_op jit(solution)/shard_map/pallas_call | solution.py:53
  73.3 0.1 collective-permute-start.17
  73.4 1.5 %collective-permute-start.18 = (bf16[16,4096]{1,0:T(8,128)(2,1)S(1)}, bf16[16,4096]{1,0:T(8,128)(2,1)S(1)}, u32[]{:S(2)}, u32[]{:S(2)}) collective-permute-start(bf16[16,4096]{1,0:T(8,128)(2,1)S(1)} %get-tuple-element.51), channel_id=1, source_target_pairs={{0,26},{1,27},{2,24},{3,25},{4,30},{5,31},{6,28},{7,29},{8,2},{9,3... | collective-permute-start | bytes 393224 | tf_op jit(solution)/shard_map/ppermute | solution.py:290
  74.8 7.2 %shard_map.108 = (bf16[2048,4096]{1,0:T(8,128)(2,1)}, f32[8,128]{1,0:T(8,128)}) custom-call(bf16[2048,128]{1,0:T(8,128)(2,1)S(1)} %get-tuple-element.54.refs_0_, bf16[128,4096]{1,0:T(8,128)(2,1)S(1)} %get-tuple-element.55.refs_1_, f32[8,128]{1,0:T(8,128)S(1)} %get-tuple-element.56.refs_2_), custom_call_target="tpu_custom_call" | custom-call | flops 4294967296 | bytes 16777216 | tf_op jit(solution)/shard_map/pallas_call | solution.py:53
  82.0 0.0 collective-permute-done.15
  82.0 0.0 collective-permute-done.17
  82.1 0.0 collective-permute-done.18
  82.1 0.7 fusion
  (7 shorter events, 0.1 us)
Async XLA Ops:
  0.6 14.6 %collective-permute-start.8 = (bf16[16,4096]{1,0:T(8,128)(2,1)}, bf16[16,4096]{1,0:T(8,128)(2,1)S(1)}, u32[]{:S(2)}, u32[]{:S(2)}) collective-permute-start(bf16[16,4096]{1,0:T(8,128)(2,1)} %bitcast.14), channel_id=1, source_target_pairs={{0,4},{1,5},{2,6},{3,7},{4,0},{5,1},{6,2},{7,3},{8,12},{9,13},{10,... | collective-permute-start | bytes 393224 | tf_op jit(solution)/shard_map/ppermute | solution.py:26
  7.3 10.0 %collective-permute-start.1 = (bf16[16,4224]{1,0:T(8,128)(2,1)S(1)}, bf16[16,4224]{1,0:T(8,128)(2,1)S(1)}, u32[]{:S(2)}, u32[]{:S(2)}) collective-permute-start(bf16[16,4224]{1,0:T(8,128)(2,1)S(1)} %pad_maximum_fusion.refs_0_), channel_id=1, source_target_pairs={{0,4},{1,5},{2,6},{3,7},{4,0},{5,1},{6,2},{7,3},{8,12},{9,13},{10,... | collective-permute-start | bytes 405512 | tf_op jit(solution)/shard_map/ppermute | solution.py:26
  7.4 10.4 %collective-permute-start.10 = (bf16[16,4096]{1,0:T(8,128)(2,1)}, bf16[16,4096]{1,0:T(8,128)(2,1)S(1)}, u32[]{:S(2)}, u32[]{:S(2)}) collective-permute-start(bf16[16,4096]{1,0:T(8,128)(2,1)} %bitcast.15), channel_id=1, source_target_pairs={{0,1},{1,0},{2,3},{3,2},{4,5},{5,4},{6,7},{7,6},{8,9},{9,8},{10,11... | collective-permute-start | bytes 393224 | tf_op jit(solution)/shard_map/ppermute | solution.py:26
  7.4 10.4 %collective-permute-start.7 = (bf16[16,4096]{1,0:T(8,128)(2,1)}, bf16[16,4096]{1,0:T(8,128)(2,1)S(1)}, u32[]{:S(2)}, u32[]{:S(2)}) collective-permute-start(bf16[16,4096]{1,0:T(8,128)(2,1)} %bitcast.16), channel_id=1, source_target_pairs={{0,2},{1,3},{2,0},{3,1},{4,6},{5,7},{6,4},{7,5},{8,10},{9,11},{10,... | collective-permute-start | bytes 393224 | tf_op jit(solution)/shard_map/ppermute | solution.py:26
  9.3 20.0 %copy-start = (bf16[1,16,4096]{2,1,0:T(8,128)(2,1)S(1)}, bf16[1,16,4096]{2,1,0:T(8,128)(2,1)}, u32[]{:S(2)}) copy-start(bf16[1,16,4096]{2,1,0:T(8,128)(2,1)} %param.7) | copy-start | bytes 393220
  15.2 6.4 %collective-permute-start.9 = (bf16[16,4096]{1,0:T(8,128)(2,1)S(1)}, bf16[16,4096]{1,0:T(8,128)(2,1)S(1)}, u32[]{:S(2)}, u32[]{:S(2)}) collective-permute-start(bf16[16,4096]{1,0:T(8,128)(2,1)S(1)} %collective-permute-done.8.refs_2_), channel_id=1, source_target_pairs={{0,2},{1,3},{2,0},{3,1},{4,6},{5,7},{6,4},{7,5},{8,10},{9,11},{10,... | collective-permute-start | bytes 393224 | tf_op jit(solution)/shard_map/ppermute | solution.py:26
  15.5 12.6 %collective-permute-start = (bf16[16,4224]{1,0:T(8,128)(2,1)S(1)}, bf16[16,4224]{1,0:T(8,128)(2,1)S(1)}, u32[]{:S(2)}, u32[]{:S(2)}) collective-permute-start(bf16[16,4224]{1,0:T(8,128)(2,1)S(1)} %pad_maximum_fusion.refs_0_), channel_id=1, source_target_pairs={{0,2},{1,3},{2,0},{3,1},{4,6},{5,7},{6,4},{7,5},{8,10},{9,11},{10,... | collective-permute-start | bytes 405512 | tf_op jit(solution)/shard_map/ppermute | solution.py:26
  17.3 11.9 %collective-permute-start.2 = (bf16[16,4224]{1,0:T(8,128)(2,1)S(1)}, bf16[16,4224]{1,0:T(8,128)(2,1)S(1)}, u32[]{:S(2)}, u32[]{:S(2)}) collective-permute-start(bf16[16,4224]{1,0:T(8,128)(2,1)S(1)} %collective-permute-done.1.refs_2_), channel_id=1, source_target_pairs={{0,2},{1,3},{2,0},{3,1},{4,6},{5,7},{6,4},{7,5},{8,10},{9,11},{10,... | collective-permute-start | bytes 405512 | tf_op jit(solution)/shard_map/ppermute | solution.py:26
  17.8 10.9 %collective-permute-start.11 = (bf16[16,4096]{1,0:T(8,128)(2,1)S(1)}, bf16[16,4096]{1,0:T(8,128)(2,1)S(1)}, u32[]{:S(2)}, u32[]{:S(2)}) collective-permute-start(bf16[16,4096]{1,0:T(8,128)(2,1)S(1)} %collective-permute-done.7.refs_1_), channel_id=1, source_target_pairs={{0,1},{1,0},{2,3},{3,2},{4,5},{5,4},{6,7},{7,6},{8,9},{9,8},{10,11... | collective-permute-start | bytes 393224 | tf_op jit(solution)/shard_map/ppermute | solution.py:26
  17.8 10.9 %collective-permute-start.12 = (bf16[16,4096]{1,0:T(8,128)(2,1)S(1)}, bf16[16,4096]{1,0:T(8,128)(2,1)S(1)}, u32[]{:S(2)}, u32[]{:S(2)}) collective-permute-start(bf16[16,4096]{1,0:T(8,128)(2,1)S(1)} %collective-permute-done.8.refs_2_), channel_id=1, source_target_pairs={{0,1},{1,0},{2,3},{3,2},{4,5},{5,4},{6,7},{7,6},{8,9},{9,8},{10,11... | collective-permute-start | bytes 393224 | tf_op jit(solution)/shard_map/ppermute | solution.py:26
  21.6 7.7 %collective-permute-start.13 = (bf16[16,4096]{1,0:T(8,128)(2,1)S(1)}, bf16[16,4096]{1,0:T(8,128)(2,1)S(1)}, u32[]{:S(2)}, u32[]{:S(2)}) collective-permute-start(bf16[16,4096]{1,0:T(8,128)(2,1)S(1)} %collective-permute-done.9.refs_3_), channel_id=1, source_target_pairs={{0,1},{1,0},{2,3},{3,2},{4,5},{5,4},{6,7},{7,6},{8,9},{9,8},{10,11... | collective-permute-start | bytes 393224 | tf_op jit(solution)/shard_map/ppermute | solution.py:26
  28.1 5.8 %collective-permute-start.3 = (bf16[16,4224]{1,0:T(8,128)(2,1)S(1)}, bf16[16,4224]{1,0:T(8,128)(2,1)S(1)}, u32[]{:S(2)}, u32[]{:S(2)}) collective-permute-start(bf16[16,4224]{1,0:T(8,128)(2,1)S(1)} %pad_maximum_fusion.refs_0_), channel_id=1, source_target_pairs={{0,1},{1,0},{2,3},{3,2},{4,5},{5,4},{6,7},{7,6},{8,9},{9,8},{10,11... | collective-permute-start | bytes 405512 | tf_op jit(solution)/shard_map/ppermute | solution.py:26
  28.7 5.2 %collective-permute-start.5 = (bf16[16,4224]{1,0:T(8,128)(2,1)S(1)}, bf16[16,4224]{1,0:T(8,128)(2,1)S(1)}, u32[]{:S(2)}, u32[]{:S(2)}) collective-permute-start(bf16[16,4224]{1,0:T(8,128)(2,1)S(1)} %collective-permute-done.1.refs_2_), channel_id=1, source_target_pairs={{0,1},{1,0},{2,3},{3,2},{4,5},{5,4},{6,7},{7,6},{8,9},{9,8},{10,11... | collective-permute-start | bytes 405512 | tf_op jit(solution)/shard_map/ppermute | solution.py:26
  28.8 5.2 %collective-permute-start.4 = (bf16[16,4224]{1,0:T(8,128)(2,1)S(1)}, bf16[16,4224]{1,0:T(8,128)(2,1)S(1)}, u32[]{:S(2)}, u32[]{:S(2)}) collective-permute-start(bf16[16,4224]{1,0:T(8,128)(2,1)S(1)} %collective-permute-done.refs_1_), channel_id=1, source_target_pairs={{0,1},{1,0},{2,3},{3,2},{4,5},{5,4},{6,7},{7,6},{8,9},{9,8},{10,11... | collective-permute-start | bytes 405512 | tf_op jit(solution)/shard_map/ppermute | solution.py:26
  29.2 4.7 %collective-permute-start.6 = (bf16[16,4224]{1,0:T(8,128)(2,1)S(1)}, bf16[16,4224]{1,0:T(8,128)(2,1)S(1)}, u32[]{:S(2)}, u32[]{:S(2)}) collective-permute-start(bf16[16,4224]{1,0:T(8,128)(2,1)S(1)} %collective-permute-done.2.refs_3_), channel_id=1, source_target_pairs={{0,1},{1,0},{2,3},{3,2},{4,5},{5,4},{6,7},{7,6},{8,9},{9,8},{10,11... | collective-permute-start | bytes 405512 | tf_op jit(solution)/shard_map/ppermute | solution.py:26
  52.3 7.1 %collective-permute-start.14 = (bf16[64,4096]{1,0:T(8,128)(2,1)S(1)}, bf16[64,4096]{1,0:T(8,128)(2,1)S(1)}, u32[]{:S(2)}, u32[]{:S(2)}) collective-permute-start(bf16[64,4096]{1,0:T(8,128)(2,1)S(1)} %get-tuple-element.39), channel_id=1, source_target_pairs={{0,1},{1,0},{2,3},{3,2},{4,5},{5,4},{6,7},{7,6},{8,9},{9,8},{10,11... | collective-permute-start | bytes 1572872 | tf_op jit(solution)/shard_map/ppermute | solution.py:26
  59.6 22.4 %collective-permute-start.15 = (bf16[16,4096]{1,0:T(8,128)(2,1)S(1)}, bf16[16,4096]{1,0:T(8,128)(2,1)S(1)}, u32[]{:S(2)}, u32[]{:S(2)}) collective-permute-start(bf16[16,4096]{1,0:T(8,128)(2,1)S(1)} %get-tuple-element.43), channel_id=1, source_target_pairs={{0,30},{1,31},{2,28},{3,29},{4,26},{5,27},{6,24},{7,25},{8,6},{9,7... | collective-permute-start | bytes 393224 | tf_op jit(solution)/shard_map/ppermute | solution.py:290
  66.1 15.9 %collective-permute-start.16 = (bf16[16,4096]{1,0:T(8,128)(2,1)S(1)}, bf16[16,4096]{1,0:T(8,128)(2,1)S(1)}, u32[]{:S(2)}, u32[]{:S(2)}) collective-permute-start(bf16[16,4096]{1,0:T(8,128)(2,1)S(1)} %get-tuple-element.44), channel_id=1, source_target_pairs={{0,24},{1,25},{2,26},{3,27},{4,28},{5,29},{6,30},{7,31},{8,0},{9,1... | collective-permute-start | bytes 393224 | tf_op jit(solution)/shard_map/ppermute | solution.py:290
  73.3 8.8 %collective-permute-start.17 = (bf16[16,4096]{1,0:T(8,128)(2,1)S(1)}, bf16[16,4096]{1,0:T(8,128)(2,1)S(1)}, u32[]{:S(2)}, u32[]{:S(2)}) collective-permute-start(bf16[16,4096]{1,0:T(8,128)(2,1)S(1)} %get-tuple-element.50), channel_id=1, source_target_pairs={{0,28},{1,29},{2,30},{3,31},{4,24},{5,25},{6,26},{7,27},{8,4},{9,5... | collective-permute-start | bytes 393224 | tf_op jit(solution)/shard_map/ppermute | solution.py:290
  73.4 8.7 %collective-permute-start.18 = (bf16[16,4096]{1,0:T(8,128)(2,1)S(1)}, bf16[16,4096]{1,0:T(8,128)(2,1)S(1)}, u32[]{:S(2)}, u32[]{:S(2)}) collective-permute-start(bf16[16,4096]{1,0:T(8,128)(2,1)S(1)} %get-tuple-element.51), channel_id=1, source_target_pairs={{0,26},{1,27},{2,24},{3,25},{4,30},{5,31},{6,28},{7,29},{8,2},{9,3... | collective-permute-start | bytes 393224 | tf_op jit(solution)/shard_map/ppermute | solution.py:290

commit v2 on v1

--- a/solution.py
+++ b/solution.py
@@ -9,7 +9,8 @@
 
 EXPERTS = 16
 LANES = 128
-SLOTS = 5
+SLOTS = 4
+STREAM = 4
 BF16, F32 = jnp.bfloat16, jnp.float32
 MIB = 1 << 20
 WHOLE = pl.BlockSpec(memory_space=pltpu.VMEM)
@@ -26,22 +27,20 @@
     return lax.ppermute(block, "expert", [(i, i ^ bits) for i in range(devices)])
 
 
-def across(block, token):
-    devices = lax.axis_size("expert")
-    found = {0: block}
-    bits = devices // 2
+def gather(block, ahead, after):
+    near = {0: block}
+    chips = lax.axis_size("expert") // 2
+    bits = chips
     while bits > 1:
-        found |= {mask | bits: swap(part, bits) for mask, part in found.items()}
-        if token is not None and bits == devices // 2:
-            found[bits], token = lax.optimization_barrier((found[bits], token))
+        near |= {mask | bits: swap(part, bits) for mask, part in near.items()}
+        if ahead is not None and bits == chips:
+            near[bits], ahead = lax.optimization_barrier((near[bits], ahead))
         bits //= 2
-    return found, token
-
-
-def gather(block, token=None):
-    near, token = across(block, token)
-    masks = sorted(near)
-    return [near[m] for m in masks] + [swap(near[m], 1) for m in masks], token
+    parts = [near[mask] for mask in sorted(near)]
+    other = [swap(part, 1) for part in parts[:-1]]
+    if after is not None:
+        parts[-1], after = lax.optimization_barrier((parts[-1], after))
+    return parts + other + [swap(parts[-1], 1)], ahead, after
 
 
 def in_hbm(array):
@@ -66,36 +65,34 @@
     return jnp.concatenate(parts, axis=0) if len(parts) > 1 else parts[0]
 
 
-def fetch_kernel(pieces, from_ref, to_ref, token_ref, sems):
+def message_kernel(grad_ref, ids_ref, gates_ref, out_ref, token_ref):
     token_ref[...] = jnp.zeros_like(token_ref)
-    rows = from_ref.shape[0] // pieces
-    parts = [pl.ds(i * rows, rows) for i in range(pieces)]
-    copies = [
-        pltpu.make_async_copy(from_ref.at[part], to_ref.at[part], sems.at[i])
-        for i, part in enumerate(parts)
-    ]
-    for copy in copies:
-        copy.start()
-    for copy in copies:
-        copy.wait()
-
-
-def fetch(weights, pieces=4):
+    rows, width = grad_ref.shape
+    out_ref[:, :width] = grad_ref[...]
+    lane = lax.broadcasted_iota(jnp.int32, (rows, LANES), 1)
+    weight = jnp.zeros((rows, LANES), F32)
+    for k in range(ids_ref.shape[1]):
+        own = ids_ref[:, k : k + 1] == lane
+        weight += jnp.where(own, gates_ref[:, k : k + 1].astype(F32), 0.0)
+    out_ref[:, width:] = weight.astype(BF16)
+
+
+def message_of(grad_out, ids, gates, beside):
+    rows, width = grad_out.shape
     return kernel_call(
-        functools.partial(fetch_kernel, pieces),
-        [in_hbm(weights)],
-        [pltpu.VMEM(weights.shape, weights.dtype), jax.ShapeDtypeStruct((8, LANES), F32)],
-        1,
-        0,
-        2 * weights.size,
-        in_specs=[pl.BlockSpec(memory_space=pltpu.HBM)],
-        scratch_shapes=[pltpu.SemaphoreType.DMA((pieces,))],
+        message_kernel,
+        [grad_out, ids, gates],
+        [jax.ShapeDtypeStruct((rows, width + LANES), BF16), jax.ShapeDtypeStruct((8, LANES), F32)],
+        4,
+        beside,
+        4 * rows * width,
     )
 
 
 def pre_kernel(count, *refs):
     pieces, refs = refs[:count], refs[count + 1 :]
-    gate_ref, up_ref, at_ref, bt_ref, xt_ref, a_ref, b_ref = refs
+    gate_ref, up_ref, at_ref, bt_ref, xt_ref, token_ref, a_ref, b_ref = refs
+    token_ref[...] = jnp.zeros_like(token_ref)
     width = gate_ref.shape[0]
     depth = min(512, width)
     for start in range(0, width, depth):
@@ -118,7 +115,7 @@
         functools.partial(pre_kernel, count),
         [*pieces, token, w_gate, w_up],
         [jax.ShapeDtypeStruct((columns, tokens), F32)] * 2
-        + [jax.ShapeDtypeStruct((width, tokens), BF16)],
+        + [jax.ShapeDtypeStruct((width, tokens), BF16), jax.ShapeDtypeStruct((8, LANES), F32)],
         6,
         4 * tokens * width * columns,
         2 * tokens * width,
@@ -134,11 +131,11 @@
     columns, width = down_ref.shape
     each, block, depth = columns // experts, downs.shape[1], gate_slots.shape[1]
     steps, turns, half = columns // block, width // depth, near_ref.shape[0]
-    ahead = SLOTS - 1
+    ahead = STREAM - 1
 
     def arrivals(ref, slots, sems, step):
         rows = pl.ds(pl.multiple_of(step * slots.shape[1], slots.shape[1]), slots.shape[1])
-        slot = lax.rem(step, SLOTS)
+        slot = lax.rem(step, STREAM)
         return pltpu.make_async_copy(ref.at[rows], slots.at[slot], sems.at[slot])
 
     def down(step):
@@ -182,7 +179,7 @@
         rows = pl.ds(pl.multiple_of(step * block, block), block)
         own = line == first + step * block // each
         weight = jnp.sum(jnp.where(own, gates, 0.0), axis=0, keepdims=True)
-        hidden_grad = weight * contract(downs[lax.rem(step, SLOTS)], c_ref[...], 1, 1)
+        hidden_grad = weight * contract(downs[lax.rem(step, STREAM)], c_ref[...], 1, 1)
         a, b = at_ref[rows, :], bt_ref[rows, :]
         g = jax.nn.sigmoid(a)
         active = a * g
@@ -199,7 +196,7 @@
         def _():
             start_pair(turn + ahead)
 
-        rows, slot = pl.ds(pl.multiple_of(turn * depth, depth), depth), lax.rem(turn, SLOTS)
+        rows, slot = pl.ds(pl.multiple_of(turn * depth, depth), depth), lax.rem(turn, STREAM)
         total = jnp.dot(gate_slots[slot], ggt_ref[...], preferred_element_type=F32)
         total += jnp.dot(up_slots[slot], ugt_ref[...], preferred_element_type=F32)
         total = total.T.astype(BF16)
@@ -221,13 +218,13 @@
         [jax.ShapeDtypeStruct((tokens, width), BF16)]
         + [jax.ShapeDtypeStruct((columns, tokens), BF16)] * 3
         + [jax.ShapeDtypeStruct((tokens // 2, width), BF16)] * 2,
-        40,
+        30,
         12 * tokens * width * columns,
         6 * width * columns,
         in_specs=[WHOLE] * (len(pieces) + 2) + [pl.BlockSpec(memory_space=pltpu.HBM)] * 3,
-        scratch_shapes=[pltpu.VMEM((SLOTS, block, width), BF16)]
-        + [pltpu.VMEM((SLOTS, depth, columns), BF16)] * 2
-        + [pltpu.SemaphoreType.DMA((SLOTS,))] * 3,
+        scratch_shapes=[pltpu.VMEM((STREAM, block, width), BF16)]
+        + [pltpu.VMEM((STREAM, depth, columns), BF16)] * 2
+        + [pltpu.SemaphoreType.DMA((STREAM,))] * 3,
     )
 
 
@@ -295,15 +292,12 @@
     experts = max(1, EXPERTS // devices)
     split = max(1, devices // EXPERTS)
     w_gate, w_up, w_down = w_gate[0], w_up[0], w_down[0]
-    chosen = expert_ids[0][:, :, None] == lax.iota(jnp.int32, LANES)
-    weight = jnp.sum(jnp.where(chosen, gates[0][:, :, None].astype(F32), 0.0), axis=1)
-    message = jnp.concatenate([grad_out[0], weight.astype(BF16)], axis=1)
-    (gate_near, token), (up_near, _) = fetch(w_gate), fetch(w_up)
-    inputs, token = gather(layer_input[0], token)
-    cotangents, _ = gather(message)
-    if devices > 8:
-        inputs, cotangents = [jnp.concatenate(inputs)], [jnp.concatenate(cotangents)]
-    at, bt, xt = pre(inputs, token, gate_near, up_near)
+    message, token = message_of(grad_out[0], expert_ids[0], gates[0], 4096 * w_gate.size)
+    inputs, token, _ = gather(layer_input[0], token, None)
+    inputs = [jnp.concatenate(inputs)] if devices > 8 else inputs
+    at, bt, xt, token = pre(inputs, token, w_gate, w_up)
+    cotangents, _, token = gather(message, None, token)
+    cotangents = [jnp.concatenate(cotangents)] if devices > 8 else cotangents
     c, ggt, ugt, ht, near, far = core(cotangents, at, bt, w_down, w_gate, w_up, experts, split)
     gate_grad, token = grads(token, (xt, ggt, 1))
     mine = (near.astype(F32) + swap(far, 1).astype(F32)).astype(BF16)

time: 83 us -> 79.5 us (0.958)
  Pallas kernels: 55.8 us -> 44.1 us
  waiting for transfers between devices: 3.32 us -> 10.9 us
  other arithmetic: 2.57 us -> 0.85 us
  local copies, waits for them, and re-layouts: 0.87 us -> 2.47 us
    pallas_call x7 -> x6, Pallas kernels: 55.8 us -> 44.1 us  [kernel_call(): pl.pallas_call(kernel, in_specs=specs, out_specs=more.pop('out_specs', [W...]
    ppermute x15, waiting for transfers between devices: 3.31 us -> 10.6 us  [swap(): lax.ppermute(block, 'expert', [(i, i ^ bits) for i in range(devices)])]
    ppermute x15, starting transfers between devices: 10.8 us -> 12.5 us  [swap(): lax.ppermute(block, 'expert', [(i, i ^ bits) for i in range(devices)])]
    squeeze x0 -> x2, local copies, waits for them, and re-layouts: none -> 1.52 us  [the longest x1 0.76 us: body(): expert_ids[0]]
    concatenate x1 -> x0, other arithmetic: 0.92 us -> none  [body(): message = jnp.concatenate([grad_out[0], weight.astype(BF16)], axis=1)]
    unnamed x2 -> x8, local copies, waits for them, and re-layouts: 0.01 us -> 0.91 us
    ppermute x4, starting transfers between devices: 8.61 us -> 7.74 us  [hand_on(): return lax.ppermute(mine, ('section', 'expert'), route)]
  transfers between devices with their start and end apart: 19 -> 19, of which waited for: 1 -> 6; matrix products, arithmetic and copies ran while one was open for 3% -> 2% of each run, Pallas kernels for 45% -> 32%
where the time goes in v2:
time: 79.5 us; the launch traced here: 79.3 us
  Pallas kernels  44.1 us (55%)
  starting transfers between devices  20.3 us (26%)
  waiting for transfers between devices  10.9 us (14%)
  local copies, waits for them, and re-layouts  2.47 us (3%)
  other arithmetic  0.85 us (1%)
    pallas_call x6, Pallas kernels, kernel_call(): pl.pallas_call(kernel, in_specs=specs, out_specs=more.pop('out_specs', [W...  44.1 us
    ppermute x15, starting transfers between devices, swap(): lax.ppermute(block, 'expert', [(i, i ^ bits) for i in range(devices)])  12.5 us
    ppermute x15, waiting for transfers between devices, swap(): lax.ppermute(block, 'expert', [(i, i ^ bits) for i in range(devices)])  10.6 us
    ppermute x4, starting transfers between devices, hand_on(): return lax.ppermute(mine, ('section', 'expert'), route)  7.74 us
  transfers between devices with their start and end apart: 19, of which 6 were waited for; matrix products, arithmetic and copies ran while one was open for 2% of the time, Pallas kernels for 32%

profile of v2, /device:TPU:0, one launch (start us, length us, event | category | flops | bytes accessed | tf_op | source)
XLA Modules:
  0.0 79.3 jit_solution(6446832170977107796)
XLA Ops:
  0.6 0.5 collective-permute-start.6
  1.1 3.7 %collective-permute-start.4 = (bf16[16,4096]{1,0:T(8,128)(2,1)}, bf16[16,4096]{1,0:T(8,128)(2,1)S(1)}, u32[]{:S(2)}, u32[]{:S(2)}) collective-permute-start(bf16[16,4096]{1,0:T(8,128)(2,1)} %bitcast.17), channel_id=1, source_target_pairs={{0,4},{1,5},{2,6},{3,7},{4,0},{5,1},{6,2},{7,3},{8,12},{9,13},{10,... | collective-permute-start | bytes 393224 | tf_op jit(solution)/shard_map/ppermute | solution.py:27
  4.8 1.6 %collective-permute-start.3 = (bf16[16,4096]{1,0:T(8,128)(2,1)}, bf16[16,4096]{1,0:T(8,128)(2,1)S(1)}, u32[]{:S(2)}, u32[]{:S(2)}) collective-permute-start(bf16[16,4096]{1,0:T(8,128)(2,1)} %bitcast.18), channel_id=1, source_target_pairs={{0,2},{1,3},{2,0},{3,1},{4,6},{5,7},{6,4},{7,5},{8,10},{9,11},{10,... | collective-permute-start | bytes 393224 | tf_op jit(solution)/shard_map/ppermute | solution.py:27
  6.4 0.8 copy.12.gates_ref
  7.1 0.8 copy.11.ids_ref
  7.9 0.9 %copy-done.3 = bf16[1,16,4096]{2,1,0:T(8,128)(2,1)S(1)} copy-done((bf16[1,16,4096]{2,1,0:T(8,128)(2,1)S(1)}, bf16[1,16,4096]{2,1,0:T(8,128)(2,1)}, u32[]{:S(2)}) %copy-start.3) | copy-done | bytes 131096
  8.8 0.1 shard_map.102
  8.9 3.1 %collective-permute-done.4.refs_2_ = bf16[16,4096]{1,0:T(8,128)(2,1)S(1)} collective-permute-done((bf16[16,4096]{1,0:T(8,128)(2,1)}, bf16[16,4096]{1,0:T(8,128)(2,1)S(1)}, u32[]{:S(2)}, u32[]{:S(2)}) %collective-permute-start.4) | collective-permute-done | bytes 131104 | tf_op jit(solution)/shard_map/ppermute | solution.py:27
  12.0 0.7 collective-permute-start.5
  12.8 3.3 %collective-permute-start.1 = (bf16[16,4224]{1,0:T(8,128)(2,1)S(1)}, bf16[16,4224]{1,0:T(8,128)(2,1)S(1)}, u32[]{:S(2)}, u32[]{:S(2)}) collective-permute-start(bf16[16,4224]{1,0:T(8,128)(2,1)S(1)} %get-tuple-element.33.refs_0_), channel_id=1, source_target_pairs={{0,4},{1,5},{2,6},{3,7},{4,0},{5,1},{6,2},{7,3},{8,12},{9,13},{10,... | collective-permute-start | bytes 405512 | tf_op jit(solution)/shard_map/ppermute | solution.py:27
  16.0 0.0 collective-permute-start
  16.0 0.0 collective-permute-done.6.refs_4_
  16.0 0.0 collective-permute-start.8
  16.1 0.0 collective-permute-done.3.refs_1_
  16.1 0.5 collective-permute-start.7
  16.6 3.5 %collective-permute-done.5.refs_3_ = bf16[16,4096]{1,0:T(8,128)(2,1)S(1)} collective-permute-done((bf16[16,4096]{1,0:T(8,128)(2,1)S(1)}, bf16[16,4096]{1,0:T(8,128)(2,1)S(1)}, u32[]{:S(2)}, u32[]{:S(2)}) %collective-permute-start.5) | collective-permute-done | bytes 131104 | tf_op jit(solution)/shard_map/ppermute | solution.py:27
  20.1 0.0 collective-permute-start.9
  20.1 2.2 %collective-permute-done.1.refs_2_ = bf16[16,4224]{1,0:T(8,128)(2,1)S(1)} collective-permute-done((bf16[16,4224]{1,0:T(8,128)(2,1)S(1)}, bf16[16,4224]{1,0:T(8,128)(2,1)S(1)}, u32[]{:S(2)}, u32[]{:S(2)}) %collective-permute-start.1) | collective-permute-done | bytes 135200 | tf_op jit(solution)/shard_map/ppermute | solution.py:27
  22.3 0.0 collective-permute-start.10
  22.3 0.6 collective-permute-done.refs_1_
  23.0 0.0 collective-permute-start.12
  23.0 0.0 collective-permute-done.8.refs_6_
  23.0 1.3 %collective-permute-start.2 = (bf16[16,4224]{1,0:T(8,128)(2,1)S(1)}, bf16[16,4224]{1,0:T(8,128)(2,1)S(1)}, u32[]{:S(2)}, u32[]{:S(2)}) collective-permute-start(bf16[16,4224]{1,0:T(8,128)(2,1)S(1)} %collective-permute-done.1.refs_2_), channel_id=1, source_target_pairs={{0,2},{1,3},{2,0},{3,1},{4,6},{5,7},{6,4},{7,5},{8,10},{9,11},{10,... | collective-permute-start | bytes 405512 | tf_op jit(solution)/shard_map/ppermute | solution.py:27
  24.3 0.0 collective-permute-done.7.refs_5_
  24.3 0.2 collective-permute-start.11
  24.5 0.0 collective-permute-done.9.refs_7_
  24.5 4.6 %shard_map.103 = (f32[2048,128]{1,0:T(8,128)S(1)}, f32[2048,128]{1,0:T(8,128)S(1)}, bf16[4096,128]{1,0:T(8,128)(2,1)S(1)}, f32[8,128]{1,0:T(8,128)S(1)}) custom-call(bf16[16,4096]{1,0:T(8,128)(2,1)S(1)} %bitcast.19, bf16[16,4096]{1,0:T(8,128)(2,1)S(1)} %collective-permute-done.3.refs_1_, bf16[16,4096]{1,0:T(8,128)(2,1)S(1)} %collective-permute-done.4.refs_2_, ...), custom_call_target="tpu_custom_call" | custom-call | flops 4294967296 | bytes 1048576 | tf_op jit(solution)/shard_map/pallas_call | solution.py:52
  29.2 0.0 collective-permute-done.2.refs_3_
  29.2 0.4 collective-permute-start.13
  29.5 0.0 collective-permute-done.10.refs_4_
  29.5 0.0 collective-permute-done.12.refs_6_
  29.5 0.0 collective-permute-done.11.refs_5_
  29.5 1.1 %collective-permute-done.13.refs_7_ = bf16[16,4224]{1,0:T(8,128)(2,1)S(1)} collective-permute-done((bf16[16,4224]{1,0:T(8,128)(2,1)S(1)}, bf16[16,4224]{1,0:T(8,128)(2,1)S(1)}, u32[]{:S(2)}, u32[]{:S(2)}) %collective-permute-start.13) | collective-permute-done | bytes 135200 | tf_op jit(solution)/shard_map/ppermute | solution.py:27
  30.6 19.0 %shard_map.104 = (bf16[128,4096]{1,0:T(8,128)(2,1)S(1)}, bf16[2048,128]{1,0:T(8,128)(2,1)S(1)}, bf16[2048,128]{1,0:T(8,128)(2,1)S(1)}, bf16[2048,128]{1,0:T(8,12...) custom-call(bf16[16,4224]{1,0:T(8,128)(2,1)S(1)} %get-tuple-element.33.refs_0_, ...), custom_call_target="tpu_custom_call" | custom-call | flops 12884901888 | bytes 50331648 | tf_op jit(solution)/shard_map/pallas_call | solution.py:52
  49.6 0.3 collective-permute-start.14
  49.9 6.6 %shard_map.105 = (bf16[4096,2048]{1,0:T(8,128)(2,1)}, f32[8,128]{1,0:T(8,128)S(1)}) custom-call(bf16[4096,128]{1,0:T(8,128)(2,1)S(1)} %get-tuple-element.43.refs_0_, bf16[2048,128]{1,0:T(8,128)(2,1)S(1)} %get-tuple-element.44.refs_1_, f32[8,128]{1,0:T(8,128)S(1)} %get-tuple-element.45.refs_2_), custom_call_target="tpu_custom_call" | custom-call | flops 4294967296 | bytes 16777216 | tf_op jit(solution)/shard_map/pallas_call | solution.py:52
  56.6 0.0 collective-permute-done.14
  56.6 0.1 add_convert_fusion
  56.7 5.3 %collective-permute-start.15 = (bf16[16,4096]{1,0:T(8,128)(2,1)S(1)}, bf16[16,4096]{1,0:T(8,128)(2,1)S(1)}, u32[]{:S(2)}, u32[]{:S(2)}) collective-permute-start(bf16[16,4096]{1,0:T(8,128)(2,1)S(1)} %get-tuple-element.47), channel_id=1, source_target_pairs={{0,30},{1,31},{2,28},{3,29},{4,26},{5,27},{6,24},{7,25},{8,6},{9,7... | collective-permute-start | bytes 393224 | tf_op jit(solution)/shard_map/ppermute | solution.py:287
  62.1 0.5 collective-permute-start.16
  62.6 6.6 %shard_map.106 = (bf16[4096,2048]{1,0:T(8,128)(2,1)}, f32[8,128]{1,0:T(8,128)S(1)}) custom-call(bf16[4096,128]{1,0:T(8,128)(2,1)S(1)} %get-tuple-element.43.refs_0_, bf16[2048,128]{1,0:T(8,128)(2,1)S(1)} %get-tuple-element.51.refs_1_, f32[8,128]{1,0:T(8,128)S(1)} %get-tuple-element.52.refs_2_), custom_call_target="tpu_custom_call" | custom-call | flops 4294967296 | bytes 16777216 | tf_op jit(solution)/shard_map/pallas_call | solution.py:52
  69.2 0.1 collective-permute-start.17
  69.3 1.9 %collective-permute-start.18 = (bf16[16,4096]{1,0:T(8,128)(2,1)S(1)}, bf16[16,4096]{1,0:T(8,128)(2,1)S(1)}, u32[]{:S(2)}, u32[]{:S(2)}) collective-permute-start(bf16[16,4096]{1,0:T(8,128)(2,1)S(1)} %get-tuple-element.55), channel_id=1, source_target_pairs={{0,26},{1,27},{2,24},{3,25},{4,30},{5,31},{6,28},{7,29},{8,2},{9,3... | collective-permute-start | bytes 393224 | tf_op jit(solution)/shard_map/ppermute | solution.py:287
  71.1 7.2 %shard_map.107 = (bf16[2048,4096]{1,0:T(8,128)(2,1)}, f32[8,128]{1,0:T(8,128)}) custom-call(bf16[2048,128]{1,0:T(8,128)(2,1)S(1)} %get-tuple-element.58.refs_0_, bf16[128,4096]{1,0:T(8,128)(2,1)S(1)} %get-tuple-element.59.refs_1_, f32[8,128]{1,0:T(8,128)S(1)} %get-tuple-element.60.refs_2_), custom_call_target="tpu_custom_call" | custom-call | flops 4294967296 | bytes 16777216 | tf_op jit(solution)/shard_map/pallas_call | solution.py:52
  78.3 0.0 collective-permute-done.15
  78.3 0.0 collective-permute-done.16
  78.3 0.3 collective-permute-done.17
  78.6 0.7 fusion
  (9 shorter events, 0.1 us)
Async XLA Ops:
  0.6 15.4 %collective-permute-start.6 = (bf16[16,4096]{1,0:T(8,128)(2,1)}, bf16[16,4096]{1,0:T(8,128)(2,1)S(1)}, u32[]{:S(2)}, u32[]{:S(2)}) collective-permute-start(bf16[16,4096]{1,0:T(8,128)(2,1)} %bitcast.16), channel_id=1, source_target_pairs={{0,1},{1,0},{2,3},{3,2},{4,5},{5,4},{6,7},{7,6},{8,9},{9,8},{10,11... | collective-permute-start | bytes 393224 | tf_op jit(solution)/shard_map/ppermute | solution.py:27
  1.1 10.9 %collective-permute-start.4 = (bf16[16,4096]{1,0:T(8,128)(2,1)}, bf16[16,4096]{1,0:T(8,128)(2,1)S(1)}, u32[]{:S(2)}, u32[]{:S(2)}) collective-permute-start(bf16[16,4096]{1,0:T(8,128)(2,1)} %bitcast.17), channel_id=1, source_target_pairs={{0,4},{1,5},{2,6},{3,7},{4,0},{5,1},{6,2},{7,3},{8,12},{9,13},{10,... | collective-permute-start | bytes 393224 | tf_op jit(solution)/shard_map/ppermute | solution.py:27
  4.8 11.2 %collective-permute-start.3 = (bf16[16,4096]{1,0:T(8,128)(2,1)}, bf16[16,4096]{1,0:T(8,128)(2,1)S(1)}, u32[]{:S(2)}, u32[]{:S(2)}) collective-permute-start(bf16[16,4096]{1,0:T(8,128)(2,1)} %bitcast.18), channel_id=1, source_target_pairs={{0,2},{1,3},{2,0},{3,1},{4,6},{5,7},{6,4},{7,5},{8,10},{9,11},{10,... | collective-permute-start | bytes 393224 | tf_op jit(solution)/shard_map/ppermute | solution.py:27
  7.9 0.9 %copy-start.3 = (bf16[1,16,4096]{2,1,0:T(8,128)(2,1)S(1)}, bf16[1,16,4096]{2,1,0:T(8,128)(2,1)}, u32[]{:S(2)}) copy-start(bf16[1,16,4096]{2,1,0:T(8,128)(2,1)} %param.11) | copy-start | bytes 393220
  8.8 15.7 %copy-start = (bf16[1,4096,2048]{2,1,0:T(8,128)(2,1)S(1)}, bf16[1,4096,2048]{2,1,0:T(8,128)(2,1)}, u32[]{:S(2)}) copy-start(bf16[1,4096,2048]{2,1,0:T(8,128)(2,1)} %param.8) | copy-start | bytes 50331652
  8.8 15.7 %copy-start.1 = (bf16[1,4096,2048]{2,1,0:T(8,128)(2,1)S(1)}, bf16[1,4096,2048]{2,1,0:T(8,128)(2,1)}, u32[]{:S(2)}) copy-start(bf16[1,4096,2048]{2,1,0:T(8,128)(2,1)} %param.9) | copy-start | bytes 50331652
  8.8 15.7 %copy-start.2 = (bf16[1,16,4096]{2,1,0:T(8,128)(2,1)S(1)}, bf16[1,16,4096]{2,1,0:T(8,128)(2,1)}, u32[]{:S(2)}) copy-start(bf16[1,16,4096]{2,1,0:T(8,128)(2,1)} %param.7) | copy-start | bytes 393220
  12.0 8.0 %collective-permute-start.5 = (bf16[16,4096]{1,0:T(8,128)(2,1)S(1)}, bf16[16,4096]{1,0:T(8,128)(2,1)S(1)}, u32[]{:S(2)}, u32[]{:S(2)}) collective-permute-start(bf16[16,4096]{1,0:T(8,128)(2,1)S(1)} %collective-permute-done.4.refs_2_), channel_id=1, source_target_pairs={{0,2},{1,3},{2,0},{3,1},{4,6},{5,7},{6,4},{7,5},{8,10},{9,11},{10,... | collective-permute-start | bytes 393224 | tf_op jit(solution)/shard_map/ppermute | solution.py:27
  12.8 9.6 %collective-permute-start.1 = (bf16[16,4224]{1,0:T(8,128)(2,1)S(1)}, bf16[16,4224]{1,0:T(8,128)(2,1)S(1)}, u32[]{:S(2)}, u32[]{:S(2)}) collective-permute-start(bf16[16,4224]{1,0:T(8,128)(2,1)S(1)} %get-tuple-element.33.refs_0_), channel_id=1, source_target_pairs={{0,4},{1,5},{2,6},{3,7},{4,0},{5,1},{6,2},{7,3},{8,12},{9,13},{10,... | collective-permute-start | bytes 405512 | tf_op jit(solution)/shard_map/ppermute | solution.py:27
  16.0 6.9 %collective-permute-start = (bf16[16,4224]{1,0:T(8,128)(2,1)S(1)}, bf16[16,4224]{1,0:T(8,128)(2,1)S(1)}, u32[]{:S(2)}, u32[]{:S(2)}) collective-permute-start(bf16[16,4224]{1,0:T(8,128)(2,1)S(1)} %get-tuple-element.33.refs_0_), channel_id=1, source_target_pairs={{0,2},{1,3},{2,0},{3,1},{4,6},{5,7},{6,4},{7,5},{8,10},{9,11},{10,... | collective-permute-start | bytes 405512 | tf_op jit(solution)/shard_map/ppermute | solution.py:27
  16.0 6.9 %collective-permute-start.8 = (bf16[16,4096]{1,0:T(8,128)(2,1)S(1)}, bf16[16,4096]{1,0:T(8,128)(2,1)S(1)}, u32[]{:S(2)}, u32[]{:S(2)}) collective-permute-start(bf16[16,4096]{1,0:T(8,128)(2,1)S(1)} %collective-permute-done.4.refs_2_), channel_id=1, source_target_pairs={{0,1},{1,0},{2,3},{3,2},{4,5},{5,4},{6,7},{7,6},{8,9},{9,8},{10,11... | collective-permute-start | bytes 393224 | tf_op jit(solution)/shard_map/ppermute | solution.py:27
  16.1 8.2 %collective-permute-start.7 = (bf16[16,4096]{1,0:T(8,128)(2,1)S(1)}, bf16[16,4096]{1,0:T(8,128)(2,1)S(1)}, u32[]{:S(2)}, u32[]{:S(2)}) collective-permute-start(bf16[16,4096]{1,0:T(8,128)(2,1)S(1)} %collective-permute-done.3.refs_1_), channel_id=1, source_target_pairs={{0,1},{1,0},{2,3},{3,2},{4,5},{5,4},{6,7},{7,6},{8,9},{9,8},{10,11... | collective-permute-start | bytes 393224 | tf_op jit(solution)/shard_map/ppermute | solution.py:27
  20.1 4.4 %collective-permute-start.9 = (bf16[16,4096]{1,0:T(8,128)(2,1)S(1)}, bf16[16,4096]{1,0:T(8,128)(2,1)S(1)}, u32[]{:S(2)}, u32[]{:S(2)}) collective-permute-start(bf16[16,4096]{1,0:T(8,128)(2,1)S(1)} %collective-permute-done.5.refs_3_), channel_id=1, source_target_pairs={{0,1},{1,0},{2,3},{3,2},{4,5},{5,4},{6,7},{7,6},{8,9},{9,8},{10,11... | collective-permute-start | bytes 393224 | tf_op jit(solution)/shard_map/ppermute | solution.py:27
  22.3 7.2 %collective-permute-start.10 = (bf16[16,4224]{1,0:T(8,128)(2,1)S(1)}, bf16[16,4224]{1,0:T(8,128)(2,1)S(1)}, u32[]{:S(2)}, u32[]{:S(2)}) collective-permute-start(bf16[16,4224]{1,0:T(8,128)(2,1)S(1)} %get-tuple-element.33.refs_0_), channel_id=1, source_target_pairs={{0,1},{1,0},{2,3},{3,2},{4,5},{5,4},{6,7},{7,6},{8,9},{9,8},{10,11... | collective-permute-start | bytes 405512 | tf_op jit(solution)/shard_map/ppermute | solution.py:27
  23.0 6.6 %collective-permute-start.12 = (bf16[16,4224]{1,0:T(8,128)(2,1)S(1)}, bf16[16,4224]{1,0:T(8,128)(2,1)S(1)}, u32[]{:S(2)}, u32[]{:S(2)}) collective-permute-start(bf16[16,4224]{1,0:T(8,128)(2,1)S(1)} %collective-permute-done.1.refs_2_), channel_id=1, source_target_pairs={{0,1},{1,0},{2,3},{3,2},{4,5},{5,4},{6,7},{7,6},{8,9},{9,8},{10,11... | collective-permute-start | bytes 405512 | tf_op jit(solution)/shard_map/ppermute | solution.py:27
  23.0 6.2 %collective-permute-start.2 = (bf16[16,4224]{1,0:T(8,128)(2,1)S(1)}, bf16[16,4224]{1,0:T(8,128)(2,1)S(1)}, u32[]{:S(2)}, u32[]{:S(2)}) collective-permute-start(bf16[16,4224]{1,0:T(8,128)(2,1)S(1)} %collective-permute-done.1.refs_2_), channel_id=1, source_target_pairs={{0,2},{1,3},{2,0},{3,1},{4,6},{5,7},{6,4},{7,5},{8,10},{9,11},{10,... | collective-permute-start | bytes 405512 | tf_op jit(solution)/shard_map/ppermute | solution.py:27
  24.3 5.3 %collective-permute-start.11 = (bf16[16,4224]{1,0:T(8,128)(2,1)S(1)}, bf16[16,4224]{1,0:T(8,128)(2,1)S(1)}, u32[]{:S(2)}, u32[]{:S(2)}) collective-permute-start(bf16[16,4224]{1,0:T(8,128)(2,1)S(1)} %collective-permute-done.refs_1_), channel_id=1, source_target_pairs={{0,1},{1,0},{2,3},{3,2},{4,5},{5,4},{6,7},{7,6},{8,9},{9,8},{10,11... | collective-permute-start | bytes 405512 | tf_op jit(solution)/shard_map/ppermute | solution.py:27
  29.2 1.4 %collective-permute-start.13 = (bf16[16,4224]{1,0:T(8,128)(2,1)S(1)}, bf16[16,4224]{1,0:T(8,128)(2,1)S(1)}, u32[]{:S(2)}, u32[]{:S(2)}) collective-permute-start(bf16[16,4224]{1,0:T(8,128)(2,1)S(1)} %collective-permute-done.2.refs_3_), channel_id=1, source_target_pairs={{0,1},{1,0},{2,3},{3,2},{4,5},{5,4},{6,7},{7,6},{8,9},{9,8},{10,11... | collective-permute-start | bytes 405512 | tf_op jit(solution)/shard_map/ppermute | solution.py:27
  49.6 7.0 %collective-permute-start.14 = (bf16[64,4096]{1,0:T(8,128)(2,1)S(1)}, bf16[64,4096]{1,0:T(8,128)(2,1)S(1)}, u32[]{:S(2)}, u32[]{:S(2)}) collective-permute-start(bf16[64,4096]{1,0:T(8,128)(2,1)S(1)} %get-tuple-element.42), channel_id=1, source_target_pairs={{0,1},{1,0},{2,3},{3,2},{4,5},{5,4},{6,7},{7,6},{8,9},{9,8},{10,11... | collective-permute-start | bytes 1572872 | tf_op jit(solution)/shard_map/ppermute | solution.py:27
  56.7 21.5 %collective-permute-start.15 = (bf16[16,4096]{1,0:T(8,128)(2,1)S(1)}, bf16[16,4096]{1,0:T(8,128)(2,1)S(1)}, u32[]{:S(2)}, u32[]{:S(2)}) collective-permute-start(bf16[16,4096]{1,0:T(8,128)(2,1)S(1)} %get-tuple-element.47), channel_id=1, source_target_pairs={{0,30},{1,31},{2,28},{3,29},{4,26},{5,27},{6,24},{7,25},{8,6},{9,7... | collective-permute-start | bytes 393224 | tf_op jit(solution)/shard_map/ppermute | solution.py:287
  62.1 16.2 %collective-permute-start.16 = (bf16[16,4096]{1,0:T(8,128)(2,1)S(1)}, bf16[16,4096]{1,0:T(8,128)(2,1)S(1)}, u32[]{:S(2)}, u32[]{:S(2)}) collective-permute-start(bf16[16,4096]{1,0:T(8,128)(2,1)S(1)} %get-tuple-element.48), channel_id=1, source_target_pairs={{0,24},{1,25},{2,26},{3,27},{4,28},{5,29},{6,30},{7,31},{8,0},{9,1... | collective-permute-start | bytes 393224 | tf_op jit(solution)/shard_map/ppermute | solution.py:287
  69.2 9.4 %collective-permute-start.17 = (bf16[16,4096]{1,0:T(8,128)(2,1)S(1)}, bf16[16,4096]{1,0:T(8,128)(2,1)S(1)}, u32[]{:S(2)}, u32[]{:S(2)}) collective-permute-start(bf16[16,4096]{1,0:T(8,128)(2,1)S(1)} %get-tuple-element.54), channel_id=1, source_target_pairs={{0,28},{1,29},{2,30},{3,31},{4,24},{5,25},{6,26},{7,27},{8,4},{9,5... | collective-permute-start | bytes 393224 | tf_op jit(solution)/shard_map/ppermute | solution.py:287
  69.3 9.3 %collective-permute-start.18 = (bf16[16,4096]{1,0:T(8,128)(2,1)S(1)}, bf16[16,4096]{1,0:T(8,128)(2,1)S(1)}, u32[]{:S(2)}, u32[]{:S(2)}) collective-permute-start(bf16[16,4096]{1,0:T(8,128)(2,1)S(1)} %get-tuple-element.55), channel_id=1, source_target_pairs={{0,26},{1,27},{2,24},{3,25},{4,30},{5,31},{6,28},{7,29},{8,2},{9,3... | collective-permute-start | bytes 393224 | tf_op jit(solution)/shard_map/ppermute | solution.py:287

commit v3 on v2

--- a/solution.py
+++ b/solution.py
@@ -304,14 +304,9 @@
     chips = devices // 2
     mine = jnp.split(mine, chips)
     far_first = sorted(range(chips), reverse=True)
-    early = [m for m in far_first if m >= chips - chips // 4 or m < chips // 4]
-    late = [m for m in far_first if m not in early]
     mine, token = lax.optimization_barrier((mine, token))
-    arrived = [hand_on(mine[m], m) for m in early]
-    up_grad, token = grads(token, (xt, ugt, 1))
-    mine, token = lax.optimization_barrier((mine, token))
-    arrived += [hand_on(mine[m], m) for m in late]
-    down_grad, _ = grads(token, (ht, c, 0))
+    arrived = [hand_on(mine[m], m) for m in far_first]
+    up_grad, down_grad, _ = grads(token, (xt, ugt, 1), (ht, c, 0))
     grad_prev = functools.reduce(jnp.add, [part.astype(F32) for part in arrived]).astype(BF16)
     return grad_prev[None], gate_grad[None], up_grad[None], down_grad[None]
 

time: 79.5 us -> 78.2 us (0.984)
  Pallas kernels: 44.1 us -> 43.1 us
    pallas_call x6 -> x5, Pallas kernels: 44.1 us -> 43.1 us  [kernel_call(): pl.pallas_call(kernel, in_specs=specs, out_specs=more.pop('out_specs', [W...]
  transfers between devices with their start and end apart: 19 -> 19, of which waited for: 6 -> 5; matrix products, arithmetic and copies ran while one was open for 2% -> 2% of each run, Pallas kernels for 32% -> 31%
where the time goes in v3:
time: 78.2 us; the launch traced here: 78 us
  Pallas kernels  43.1 us (55%)
  starting transfers between devices  20.2 us (26%)
  waiting for transfers between devices  10.6 us (14%)
  local copies, waits for them, and re-layouts  2.47 us (3%)
  other arithmetic  0.85 us (1%)
    pallas_call x5, Pallas kernels, kernel_call(): pl.pallas_call(kernel, in_specs=specs, out_specs=more.pop('out_specs', [W...  43.1 us
    ppermute x15, starting transfers between devices, swap(): lax.ppermute(block, 'expert', [(i, i ^ bits) for i in range(devices)])  12.5 us
    ppermute x15, waiting for transfers between devices, swap(): lax.ppermute(block, 'expert', [(i, i ^ bits) for i in range(devices)])  10.6 us
    ppermute x4, starting transfers between devices, hand_on(): return lax.ppermute(mine, ('section', 'expert'), route)  7.7 us
  transfers between devices with their start and end apart: 19, of which 5 were waited for; matrix products, arithmetic and copies ran while one was open for 2% of the time, Pallas kernels for 31%

profile of v3, /device:TPU:0, one launch (start us, length us, event | category | flops | bytes accessed | tf_op | source)
XLA Modules:
  0.0 78.0 jit_solution(2317386708044648750)
XLA Ops:
  0.6 0.5 collective-permute-start.6
  1.1 3.7 %collective-permute-start.4 = (bf16[16,4096]{1,0:T(8,128)(2,1)}, bf16[16,4096]{1,0:T(8,128)(2,1)S(1)}, u32[]{:S(2)}, u32[]{:S(2)}) collective-permute-start(bf16[16,4096]{1,0:T(8,128)(2,1)} %bitcast.17), channel_id=1, source_target_pairs={{0,4},{1,5},{2,6},{3,7},{4,0},{5,1},{6,2},{7,3},{8,12},{9,13},{10,... | collective-permute-start | bytes 393224 | tf_op jit(solution)/shard_map/ppermute | solution.py:27
  4.8 1.6 %collective-permute-start.3 = (bf16[16,4096]{1,0:T(8,128)(2,1)}, bf16[16,4096]{1,0:T(8,128)(2,1)S(1)}, u32[]{:S(2)}, u32[]{:S(2)}) collective-permute-start(bf16[16,4096]{1,0:T(8,128)(2,1)} %bitcast.18), channel_id=1, source_target_pairs={{0,2},{1,3},{2,0},{3,1},{4,6},{5,7},{6,4},{7,5},{8,10},{9,11},{10,... | collective-permute-start | bytes 393224 | tf_op jit(solution)/shard_map/ppermute | solution.py:27
  6.4 0.8 copy.12.gates_ref
  7.1 0.8 copy.11.ids_ref
  7.9 0.9 %copy-done.3 = bf16[1,16,4096]{2,1,0:T(8,128)(2,1)S(1)} copy-done((bf16[1,16,4096]{2,1,0:T(8,128)(2,1)S(1)}, bf16[1,16,4096]{2,1,0:T(8,128)(2,1)}, u32[]{:S(2)}) %copy-start.3) | copy-done | bytes 131096
  8.8 0.1 shard_map.102
  8.9 3.1 %collective-permute-done.4.refs_2_ = bf16[16,4096]{1,0:T(8,128)(2,1)S(1)} collective-permute-done((bf16[16,4096]{1,0:T(8,128)(2,1)}, bf16[16,4096]{1,0:T(8,128)(2,1)S(1)}, u32[]{:S(2)}, u32[]{:S(2)}) %collective-permute-start.4) | collective-permute-done | bytes 131104 | tf_op jit(solution)/shard_map/ppermute | solution.py:27
  12.0 0.7 collective-permute-start.5
  12.8 3.3 %collective-permute-start.1 = (bf16[16,4224]{1,0:T(8,128)(2,1)S(1)}, bf16[16,4224]{1,0:T(8,128)(2,1)S(1)}, u32[]{:S(2)}, u32[]{:S(2)}) collective-permute-start(bf16[16,4224]{1,0:T(8,128)(2,1)S(1)} %get-tuple-element.29.refs_0_), channel_id=1, source_target_pairs={{0,4},{1,5},{2,6},{3,7},{4,0},{5,1},{6,2},{7,3},{8,12},{9,13},{10,... | collective-permute-start | bytes 405512 | tf_op jit(solution)/shard_map/ppermute | solution.py:27
  16.0 0.0 collective-permute-start
  16.0 0.0 collective-permute-done.6.refs_4_
  16.0 0.0 collective-permute-start.8
  16.1 0.0 collective-permute-done.3.refs_1_
  16.1 0.5 collective-permute-start.7
  16.6 3.5 %collective-permute-done.5.refs_3_ = bf16[16,4096]{1,0:T(8,128)(2,1)S(1)} collective-permute-done((bf16[16,4096]{1,0:T(8,128)(2,1)S(1)}, bf16[16,4096]{1,0:T(8,128)(2,1)S(1)}, u32[]{:S(2)}, u32[]{:S(2)}) %collective-permute-start.5) | collective-permute-done | bytes 131104 | tf_op jit(solution)/shard_map/ppermute | solution.py:27
  20.1 0.0 collective-permute-start.9
  20.1 2.2 %collective-permute-done.1.refs_2_ = bf16[16,4224]{1,0:T(8,128)(2,1)S(1)} collective-permute-done((bf16[16,4224]{1,0:T(8,128)(2,1)S(1)}, bf16[16,4224]{1,0:T(8,128)(2,1)S(1)}, u32[]{:S(2)}, u32[]{:S(2)}) %collective-permute-start.1) | collective-permute-done | bytes 135200 | tf_op jit(solution)/shard_map/ppermute | solution.py:27
  22.3 0.0 collective-permute-start.10
  22.3 0.6 collective-permute-done.refs_1_
  23.0 0.0 collective-permute-start.12
  23.0 0.0 collective-permute-done.8.refs_6_
  23.0 1.3 %collective-permute-start.2 = (bf16[16,4224]{1,0:T(8,128)(2,1)S(1)}, bf16[16,4224]{1,0:T(8,128)(2,1)S(1)}, u32[]{:S(2)}, u32[]{:S(2)}) collective-permute-start(bf16[16,4224]{1,0:T(8,128)(2,1)S(1)} %collective-permute-done.1.refs_2_), channel_id=1, source_target_pairs={{0,2},{1,3},{2,0},{3,1},{4,6},{5,7},{6,4},{7,5},{8,10},{9,11},{10,... | collective-permute-start | bytes 405512 | tf_op jit(solution)/shard_map/ppermute | solution.py:27
  24.3 0.0 collective-permute-done.7.refs_5_
  24.3 0.2 collective-permute-start.11
  24.5 0.0 collective-permute-done.9.refs_7_
  24.5 4.6 %shard_map.103 = (f32[2048,128]{1,0:T(8,128)S(1)}, f32[2048,128]{1,0:T(8,128)S(1)}, bf16[4096,128]{1,0:T(8,128)(2,1)S(1)}, f32[8,128]{1,0:T(8,128)S(1)}) custom-call(bf16[16,4096]{1,0:T(8,128)(2,1)S(1)} %bitcast.19, bf16[16,4096]{1,0:T(8,128)(2,1)S(1)} %collective-permute-done.3.refs_1_, bf16[16,4096]{1,0:T(8,128)(2,1)S(1)} %collective-permute-done.4.refs_2_, ...), custom_call_target="tpu_custom_call" | custom-call | flops 4294967296 | bytes 1048576 | tf_op jit(solution)/shard_map/pallas_call | solution.py:52
  29.2 0.0 collective-permute-done.2.refs_3_
  29.2 0.4 collective-permute-start.13
  29.5 0.0 collective-permute-done.10.refs_4_
  29.5 0.0 collective-permute-done.12.refs_6_
  29.5 0.0 collective-permute-done.11.refs_5_
  29.5 1.1 %collective-permute-done.13.refs_7_ = bf16[16,4224]{1,0:T(8,128)(2,1)S(1)} collective-permute-done((bf16[16,4224]{1,0:T(8,128)(2,1)S(1)}, bf16[16,4224]{1,0:T(8,128)(2,1)S(1)}, u32[]{:S(2)}, u32[]{:S(2)}) %collective-permute-start.13) | collective-permute-done | bytes 135200 | tf_op jit(solution)/shard_map/ppermute | solution.py:27
  30.6 19.0 %shard_map.104 = (bf16[128,4096]{1,0:T(8,128)(2,1)S(1)}, bf16[2048,128]{1,0:T(8,128)(2,1)S(1)}, bf16[2048,128]{1,0:T(8,128)(2,1)S(1)}, bf16[2048,128]{1,0:T(8,12...) custom-call(bf16[16,4224]{1,0:T(8,128)(2,1)S(1)} %get-tuple-element.29.refs_0_, ...), custom_call_target="tpu_custom_call" | custom-call | flops 12884901888 | bytes 50331648 | tf_op jit(solution)/shard_map/pallas_call | solution.py:52
  49.6 0.3 collective-permute-start.14
  49.9 6.6 %shard_map.105 = (bf16[4096,2048]{1,0:T(8,128)(2,1)}, f32[8,128]{1,0:T(8,128)S(1)}) custom-call(bf16[4096,128]{1,0:T(8,128)(2,1)S(1)} %get-tuple-element.39.refs_0_, bf16[2048,128]{1,0:T(8,128)(2,1)S(1)} %get-tuple-element.40.refs_1_, f32[8,128]{1,0:T(8,128)S(1)} %get-tuple-element.41.refs_2_), custom_call_target="tpu_custom_call" | custom-call | flops 4294967296 | bytes 16777216 | tf_op jit(solution)/shard_map/pallas_call | solution.py:52
  56.6 0.0 collective-permute-done.14
  56.6 0.1 add_convert_fusion
  56.7 5.3 %collective-permute-start.15 = (bf16[16,4096]{1,0:T(8,128)(2,1)S(1)}, bf16[16,4096]{1,0:T(8,128)(2,1)S(1)}, u32[]{:S(2)}, u32[]{:S(2)}) collective-permute-start(bf16[16,4096]{1,0:T(8,128)(2,1)S(1)} %get-tuple-element.43), channel_id=1, source_target_pairs={{0,30},{1,31},{2,28},{3,29},{4,26},{5,27},{6,24},{7,25},{8,6},{9,7... | collective-permute-start | bytes 393224 | tf_op jit(solution)/shard_map/ppermute | solution.py:287
  62.1 0.0 collective-permute-start.16
  62.1 1.8 %collective-permute-start.17 = (bf16[16,4096]{1,0:T(8,128)(2,1)S(1)}, bf16[16,4096]{1,0:T(8,128)(2,1)S(1)}, u32[]{:S(2)}, u32[]{:S(2)}) collective-permute-start(bf16[16,4096]{1,0:T(8,128)(2,1)S(1)} %get-tuple-element.45), channel_id=1, source_target_pairs={{0,26},{1,27},{2,24},{3,25},{4,30},{5,31},{6,28},{7,29},{8,2},{9,3... | collective-permute-start | bytes 393224 | tf_op jit(solution)/shard_map/ppermute | solution.py:287
  63.9 0.5 collective-permute-start.18
  64.4 12.8 %shard_map.106 = (bf16[4096,2048]{1,0:T(8,128)(2,1)}, bf16[2048,4096]{1,0:T(8,128)(2,1)}, f32[8,128]{1,0:T(8,128)}) custom-call(bf16[4096,128]{1,0:T(8,128)(2,1)S(1)} %get-tuple-element.39.refs_0_, bf16[2048,128]{1,0:T(8,128)(2,1)S(1)} %get-tuple-element.48.refs_1_, bf16[2048,128]{1,0:T(8,128)(2,1)S(1)} %get-tuple-element.49.refs_2_, ...), custom_call_target="tpu_custom_call" | custom-call | flops 8589934592 | bytes 33554432 | tf_op jit(solution)/shard_map/pallas_call | solution.py:52
  77.2 0.0 collective-permute-done.15
  77.2 0.0 collective-permute-done.16
  77.2 0.0 collective-permute-done.17
  77.2 0.0 collective-permute-done.18
  77.3 0.7 fusion
  (8 shorter events, 0.0 us)
Async XLA Ops:
  0.6 15.4 %collective-permute-start.6 = (bf16[16,4096]{1,0:T(8,128)(2,1)}, bf16[16,4096]{1,0:T(8,128)(2,1)S(1)}, u32[]{:S(2)}, u32[]{:S(2)}) collective-permute-start(bf16[16,4096]{1,0:T(8,128)(2,1)} %bitcast.16), channel_id=1, source_target_pairs={{0,1},{1,0},{2,3},{3,2},{4,5},{5,4},{6,7},{7,6},{8,9},{9,8},{10,11... | collective-permute-start | bytes 393224 | tf_op jit(solution)/shard_map/ppermute | solution.py:27
  1.1 10.9 %collective-permute-start.4 = (bf16[16,4096]{1,0:T(8,128)(2,1)}, bf16[16,4096]{1,0:T(8,128)(2,1)S(1)}, u32[]{:S(2)}, u32[]{:S(2)}) collective-permute-start(bf16[16,4096]{1,0:T(8,128)(2,1)} %bitcast.17), channel_id=1, source_target_pairs={{0,4},{1,5},{2,6},{3,7},{4,0},{5,1},{6,2},{7,3},{8,12},{9,13},{10,... | collective-permute-start | bytes 393224 | tf_op jit(solution)/shard_map/ppermute | solution.py:27
  4.8 11.2 %collective-permute-start.3 = (bf16[16,4096]{1,0:T(8,128)(2,1)}, bf16[16,4096]{1,0:T(8,128)(2,1)S(1)}, u32[]{:S(2)}, u32[]{:S(2)}) collective-permute-start(bf16[16,4096]{1,0:T(8,128)(2,1)} %bitcast.18), channel_id=1, source_target_pairs={{0,2},{1,3},{2,0},{3,1},{4,6},{5,7},{6,4},{7,5},{8,10},{9,11},{10,... | collective-permute-start | bytes 393224 | tf_op jit(solution)/shard_map/ppermute | solution.py:27
  7.9 0.9 %copy-start.3 = (bf16[1,16,4096]{2,1,0:T(8,128)(2,1)S(1)}, bf16[1,16,4096]{2,1,0:T(8,128)(2,1)}, u32[]{:S(2)}) copy-start(bf16[1,16,4096]{2,1,0:T(8,128)(2,1)} %param.11) | copy-start | bytes 393220
  8.8 15.7 %copy-start = (bf16[1,4096,2048]{2,1,0:T(8,128)(2,1)S(1)}, bf16[1,4096,2048]{2,1,0:T(8,128)(2,1)}, u32[]{:S(2)}) copy-start(bf16[1,4096,2048]{2,1,0:T(8,128)(2,1)} %param.8) | copy-start | bytes 50331652
  8.8 15.7 %copy-start.1 = (bf16[1,4096,2048]{2,1,0:T(8,128)(2,1)S(1)}, bf16[1,4096,2048]{2,1,0:T(8,128)(2,1)}, u32[]{:S(2)}) copy-start(bf16[1,4096,2048]{2,1,0:T(8,128)(2,1)} %param.9) | copy-start | bytes 50331652
  8.8 15.7 %copy-start.2 = (bf16[1,16,4096]{2,1,0:T(8,128)(2,1)S(1)}, bf16[1,16,4096]{2,1,0:T(8,128)(2,1)}, u32[]{:S(2)}) copy-start(bf16[1,16,4096]{2,1,0:T(8,128)(2,1)} %param.7) | copy-start | bytes 393220
  12.0 8.0 %collective-permute-start.5 = (bf16[16,4096]{1,0:T(8,128)(2,1)S(1)}, bf16[16,4096]{1,0:T(8,128)(2,1)S(1)}, u32[]{:S(2)}, u32[]{:S(2)}) collective-permute-start(bf16[16,4096]{1,0:T(8,128)(2,1)S(1)} %collective-permute-done.4.refs_2_), channel_id=1, source_target_pairs={{0,2},{1,3},{2,0},{3,1},{4,6},{5,7},{6,4},{7,5},{8,10},{9,11},{10,... | collective-permute-start | bytes 393224 | tf_op jit(solution)/shard_map/ppermute | solution.py:27
  12.8 9.6 %collective-permute-start.1 = (bf16[16,4224]{1,0:T(8,128)(2,1)S(1)}, bf16[16,4224]{1,0:T(8,128)(2,1)S(1)}, u32[]{:S(2)}, u32[]{:S(2)}) collective-permute-start(bf16[16,4224]{1,0:T(8,128)(2,1)S(1)} %get-tuple-element.29.refs_0_), channel_id=1, source_target_pairs={{0,4},{1,5},{2,6},{3,7},{4,0},{5,1},{6,2},{7,3},{8,12},{9,13},{10,... | collective-permute-start | bytes 405512 | tf_op jit(solution)/shard_map/ppermute | solution.py:27
  16.0 6.9 %collective-permute-start = (bf16[16,4224]{1,0:T(8,128)(2,1)S(1)}, bf16[16,4224]{1,0:T(8,128)(2,1)S(1)}, u32[]{:S(2)}, u32[]{:S(2)}) collective-permute-start(bf16[16,4224]{1,0:T(8,128)(2,1)S(1)} %get-tuple-element.29.refs_0_), channel_id=1, source_target_pairs={{0,2},{1,3},{2,0},{3,1},{4,6},{5,7},{6,4},{7,5},{8,10},{9,11},{10,... | collective-permute-start | bytes 405512 | tf_op jit(solution)/shard_map/ppermute | solution.py:27
  16.0 6.9 %collective-permute-start.8 = (bf16[16,4096]{1,0:T(8,128)(2,1)S(1)}, bf16[16,4096]{1,0:T(8,128)(2,1)S(1)}, u32[]{:S(2)}, u32[]{:S(2)}) collective-permute-start(bf16[16,4096]{1,0:T(8,128)(2,1)S(1)} %collective-permute-done.4.refs_2_), channel_id=1, source_target_pairs={{0,1},{1,0},{2,3},{3,2},{4,5},{5,4},{6,7},{7,6},{8,9},{9,8},{10,11... | collective-permute-start | bytes 393224 | tf_op jit(solution)/shard_map/ppermute | solution.py:27
  16.1 8.2 %collective-permute-start.7 = (bf16[16,4096]{1,0:T(8,128)(2,1)S(1)}, bf16[16,4096]{1,0:T(8,128)(2,1)S(1)}, u32[]{:S(2)}, u32[]{:S(2)}) collective-permute-start(bf16[16,4096]{1,0:T(8,128)(2,1)S(1)} %collective-permute-done.3.refs_1_), channel_id=1, source_target_pairs={{0,1},{1,0},{2,3},{3,2},{4,5},{5,4},{6,7},{7,6},{8,9},{9,8},{10,11... | collective-permute-start | bytes 393224 | tf_op jit(solution)/shard_map/ppermute | solution.py:27
  20.1 4.4 %collective-permute-start.9 = (bf16[16,4096]{1,0:T(8,128)(2,1)S(1)}, bf16[16,4096]{1,0:T(8,128)(2,1)S(1)}, u32[]{:S(2)}, u32[]{:S(2)}) collective-permute-start(bf16[16,4096]{1,0:T(8,128)(2,1)S(1)} %collective-permute-done.5.refs_3_), channel_id=1, source_target_pairs={{0,1},{1,0},{2,3},{3,2},{4,5},{5,4},{6,7},{7,6},{8,9},{9,8},{10,11... | collective-permute-start | bytes 393224 | tf_op jit(solution)/shard_map/ppermute | solution.py:27
  22.3 7.2 %collective-permute-start.10 = (bf16[16,4224]{1,0:T(8,128)(2,1)S(1)}, bf16[16,4224]{1,0:T(8,128)(2,1)S(1)}, u32[]{:S(2)}, u32[]{:S(2)}) collective-permute-start(bf16[16,4224]{1,0:T(8,128)(2,1)S(1)} %get-tuple-element.29.refs_0_), channel_id=1, source_target_pairs={{0,1},{1,0},{2,3},{3,2},{4,5},{5,4},{6,7},{7,6},{8,9},{9,8},{10,11... | collective-permute-start | bytes 405512 | tf_op jit(solution)/shard_map/ppermute | solution.py:27
  23.0 6.6 %collective-permute-start.12 = (bf16[16,4224]{1,0:T(8,128)(2,1)S(1)}, bf16[16,4224]{1,0:T(8,128)(2,1)S(1)}, u32[]{:S(2)}, u32[]{:S(2)}) collective-permute-start(bf16[16,4224]{1,0:T(8,128)(2,1)S(1)} %collective-permute-done.1.refs_2_), channel_id=1, source_target_pairs={{0,1},{1,0},{2,3},{3,2},{4,5},{5,4},{6,7},{7,6},{8,9},{9,8},{10,11... | collective-permute-start | bytes 405512 | tf_op jit(solution)/shard_map/ppermute | solution.py:27
  23.0 6.2 %collective-permute-start.2 = (bf16[16,4224]{1,0:T(8,128)(2,1)S(1)}, bf16[16,4224]{1,0:T(8,128)(2,1)S(1)}, u32[]{:S(2)}, u32[]{:S(2)}) collective-permute-start(bf16[16,4224]{1,0:T(8,128)(2,1)S(1)} %collective-permute-done.1.refs_2_), channel_id=1, source_target_pairs={{0,2},{1,3},{2,0},{3,1},{4,6},{5,7},{6,4},{7,5},{8,10},{9,11},{10,... | collective-permute-start | bytes 405512 | tf_op jit(solution)/shard_map/ppermute | solution.py:27
  24.3 5.3 %collective-permute-start.11 = (bf16[16,4224]{1,0:T(8,128)(2,1)S(1)}, bf16[16,4224]{1,0:T(8,128)(2,1)S(1)}, u32[]{:S(2)}, u32[]{:S(2)}) collective-permute-start(bf16[16,4224]{1,0:T(8,128)(2,1)S(1)} %collective-permute-done.refs_1_), channel_id=1, source_target_pairs={{0,1},{1,0},{2,3},{3,2},{4,5},{5,4},{6,7},{7,6},{8,9},{9,8},{10,11... | collective-permute-start | bytes 405512 | tf_op jit(solution)/shard_map/ppermute | solution.py:27
  29.2 1.4 %collective-permute-start.13 = (bf16[16,4224]{1,0:T(8,128)(2,1)S(1)}, bf16[16,4224]{1,0:T(8,128)(2,1)S(1)}, u32[]{:S(2)}, u32[]{:S(2)}) collective-permute-start(bf16[16,4224]{1,0:T(8,128)(2,1)S(1)} %collective-permute-done.2.refs_3_), channel_id=1, source_target_pairs={{0,1},{1,0},{2,3},{3,2},{4,5},{5,4},{6,7},{7,6},{8,9},{9,8},{10,11... | collective-permute-start | bytes 405512 | tf_op jit(solution)/shard_map/ppermute | solution.py:27
  49.6 7.0 %collective-permute-start.14 = (bf16[64,4096]{1,0:T(8,128)(2,1)S(1)}, bf16[64,4096]{1,0:T(8,128)(2,1)S(1)}, u32[]{:S(2)}, u32[]{:S(2)}) collective-permute-start(bf16[64,4096]{1,0:T(8,128)(2,1)S(1)} %get-tuple-element.38), channel_id=1, source_target_pairs={{0,1},{1,0},{2,3},{3,2},{4,5},{5,4},{6,7},{7,6},{8,9},{9,8},{10,11... | collective-permute-start | bytes 1572872 | tf_op jit(solution)/shard_map/ppermute | solution.py:27
  56.7 20.5 %collective-permute-start.15 = (bf16[16,4096]{1,0:T(8,128)(2,1)S(1)}, bf16[16,4096]{1,0:T(8,128)(2,1)S(1)}, u32[]{:S(2)}, u32[]{:S(2)}) collective-permute-start(bf16[16,4096]{1,0:T(8,128)(2,1)S(1)} %get-tuple-element.43), channel_id=1, source_target_pairs={{0,30},{1,31},{2,28},{3,29},{4,26},{5,27},{6,24},{7,25},{8,6},{9,7... | collective-permute-start | bytes 393224 | tf_op jit(solution)/shard_map/ppermute | solution.py:287
  62.1 15.2 %collective-permute-start.16 = (bf16[16,4096]{1,0:T(8,128)(2,1)S(1)}, bf16[16,4096]{1,0:T(8,128)(2,1)S(1)}, u32[]{:S(2)}, u32[]{:S(2)}) collective-permute-start(bf16[16,4096]{1,0:T(8,128)(2,1)S(1)} %get-tuple-element.44), channel_id=1, source_target_pairs={{0,28},{1,29},{2,30},{3,31},{4,24},{5,25},{6,26},{7,27},{8,4},{9,5... | collective-permute-start | bytes 393224 | tf_op jit(solution)/shard_map/ppermute | solution.py:287
  62.1 15.2 %collective-permute-start.17 = (bf16[16,4096]{1,0:T(8,128)(2,1)S(1)}, bf16[16,4096]{1,0:T(8,128)(2,1)S(1)}, u32[]{:S(2)}, u32[]{:S(2)}) collective-permute-start(bf16[16,4096]{1,0:T(8,128)(2,1)S(1)} %get-tuple-element.45), channel_id=1, source_target_pairs={{0,26},{1,27},{2,24},{3,25},{4,30},{5,31},{6,28},{7,29},{8,2},{9,3... | collective-permute-start | bytes 393224 | tf_op jit(solution)/shard_map/ppermute | solution.py:287
  63.9 13.3 %collective-permute-start.18 = (bf16[16,4096]{1,0:T(8,128)(2,1)S(1)}, bf16[16,4096]{1,0:T(8,128)(2,1)S(1)}, u32[]{:S(2)}, u32[]{:S(2)}) collective-permute-start(bf16[16,4096]{1,0:T(8,128)(2,1)S(1)} %get-tuple-element.46), channel_id=1, source_target_pairs={{0,24},{1,25},{2,26},{3,27},{4,28},{5,29},{6,30},{7,31},{8,0},{9,1... | collective-permute-start | bytes 393224 | tf_op jit(solution)/shard_map/ppermute | solution.py:287
